TPU v7x, 32 devices: a whole 2x2x4 slice. The times are simulated.
32 devices in a mesh: rep: 8 (over z, x), grp: 4 (over y, core).
Axes of the slice: x: 2, y: 2, z: 4, core: 2. Of those that a mesh axis runs over, the one named last changes fastest.
Arguments:
- tokens: bfloat16 [8, 2048, 768], P('rep', 'grp'), may hold values from -6 to 6
- segment_ids: int32 [8, 2048], P('rep'), may hold values from 0 to 9, as said below
- w_qkv: bfloat16 [768, 2304], P('grp'), may hold values from -0.21875 to 0.21875
- w_out: bfloat16 [768, 768], P('grp'), may hold values from -1.75 to 1.75
- w_up: bfloat16 [768, 3072], P('grp'), may hold values from -0.21875 to 0.21875
- w_down: bfloat16 [3072, 768], P('grp'), may hold values from -0.109375 to 0.109375
- norm_gains: float32 [2, 768], replicated, may hold values from 0.5 to 1.5
- norm_shifts: float32 [2, 768], replicated, may hold values from -1.2 to 1.2
- proj_biases: float32 [4, 768], replicated, may hold values from -1.2 to 1.2
- up_bias: float32 [3072], replicated, may hold values from -1.8 to 1.8
- cotangent: bfloat16 [8, 2048, 768], P('rep', 'grp'), may hold values from -6 to 6
Outputs:
- block_out: bfloat16 [8, 2048, 768], P('rep', 'grp')
- input_grad: float32 [8, 2048, 768], P('rep', 'grp')
- grad_qkv: float32 [768, 2304], P('grp')
- grad_out: float32 [768, 768], P('grp')
- grad_up: float32 [768, 3072], P('grp')
- grad_down: float32 [3072, 768], P('grp')
- grad_gains: float32 [2, 768], replicated
- grad_shifts: float32 [2, 768], replicated
- grad_biases: float32 [4, 768], replicated
- grad_up_bias: float32 [3072], replicated
Inputs may be any that keep to these rules, and one draw needn't show every extreme that they name: `segment_ids`: in each sequence the ids start at 0 and never fall. In one sequence, drawn from the seed, there are three documents and the middle one begins within the first 512 tokens and ends within the last 512; in the others there are ten documents, each but the last of 102 to 204 tokens.
All inputs are finite; a program needn't handle non-finite values.
Results may differ from a plain program's by a relative error of at most 0.017.
Values may be sent and summed in bfloat16 or wider, within the bound.
No kernel may reach another device: no remote copies, remote signals or barrier semaphores. Data moves between devices by JAX's collectives and lax.ppermute only.
A program may use at most 128 MiB of HBM per device.

v0:
```python
import functools
import math

import jax
import jax.numpy as jnp
from jax import lax
from jax.experimental import pallas as pl
from jax.experimental.pallas import tpu as pltpu
from jax.sharding import PartitionSpec as P

D = 768
H = 12
HD = 64
FF = 3072
PAIRS = H // 2
LANES = 2 * HD
NEG = -1e30
SCALE = 1.0 / math.sqrt(HD)
F32 = jnp.float32
BF16 = jnp.bfloat16


def layer_norm(values, gain_row, shift_row):
    centre = values - jnp.mean(values, axis=-1, keepdims=True)
    spread = jnp.mean(centre * centre, axis=-1, keepdims=True)
    return centre * lax.rsqrt(spread + 1e-05) * gain_row + shift_row


def add_rows(left, piece):
    return jnp.dot(left, piece, preferred_element_type=F32)


def back_rows(right, piece):
    return jnp.einsum("te,ce->tc", right, piece, preferred_element_type=F32)


def token_product(left, right):
    return jnp.einsum("tc,te->ce", left, right, preferred_element_type=F32)


def after(value, *others):
    return lax.optimization_barrier((value,) + others)[0]


def swap(value, axis, size, mask, *until):
    got = lax.ppermute(value, axis, [(i, i ^ mask) for i in range(size)])
    return after(got, *until) if until else got


def bits_of(size):
    return size.bit_length() - 1


def gather_pieces(value, size, later, until_far, until_core):
    pieces = [value]
    for bit in range(1, bits_of(size)):
        mask = 1 << bit
        pairs = [(i, i ^ mask) for i in range(size) if i & mask or not later]
        pieces += [after(lax.ppermute(piece, "grp", pairs), *until_far) for piece in pieces]
    sent = [after(value, *until_far)] + pieces[1:] if later else pieces
    return pieces + [swap(piece, "grp", size, 1, *until_core) for piece in sent]


def block_place(block, me, size):
    near = block ^ me
    return (near >> 1) | ((near & 1) << (bits_of(size) - 1))


def far_rows(weight, rep, size, reps, spread, before, y_until, x_until):
    rows = weight.shape[0]
    side = rep & 1
    half = rows // 2
    spread = spread and half % 16 == 0
    pieces = [(0, 0, weight)]
    for bit in range(1, bits_of(size)):
        mask = 1 << bit
        found = []
        for near, first, piece in pieces:
            if spread and near == 0:
                part = lax.dynamic_slice_in_dim(piece, side * half, half, 0)
                got = swap(after(part, *before), "grp", size, mask, *y_until)
                found.append((near | mask, side * half, got))
                found.append((near | mask, (1 - side) * half, swap(got, "rep", reps, 1, *x_until)))
            else:
                found.append((near | mask, first, swap(after(piece, *before), "grp", size, mask, *y_until)))
        pieces = pieces + found
    return pieces


def both_cores(pieces, own_other, size, me, rows, until=()):
    starts, found = [], []
    for near, first, piece in pieces:
        starts += [(me ^ near) * rows + first, (me ^ near ^ 1) * rows + first]
        other = own_other if near == 0 else swap(piece, "grp", size, 1, *until)
        found += [piece, other]
    return starts, found


def place_kernel(counts, columns, starts, *refs):
    pieces, (out, sem) = refs[:-2], refs[-2:]
    copies = []
    for i, count in enumerate(counts):
        start = pl.multiple_of(starts[i] * 16, 16)
        for source, target, width in columns:
            copies.append(
                pltpu.make_async_copy(
                    pieces[i].at[:, pl.ds(source, width)],
                    out.at[pl.ds(start, count), pl.ds(target, width)],
                    sem.at[len(copies)],
                )
            )
    for copy in copies:
        copy.start()
    for copy in copies:
        copy.wait()


def place_rows(weight, size, starts, pieces, columns=None):
    rows, width = weight.shape
    counts = [piece.shape[0] for piece in pieces]
    columns = columns or [(0, 0, width)]
    anywhere = pl.BlockSpec(memory_space=pl.ANY)
    return pl.pallas_call(
        functools.partial(place_kernel, counts, columns),
        grid_spec=pltpu.PrefetchScalarGridSpec(
            num_scalar_prefetch=1,
            grid=(1,),
            in_specs=[anywhere] * len(pieces),
            out_specs=pl.BlockSpec((size * rows, width), lambda i, starts: (0, 0)),
            scratch_shapes=[pltpu.SemaphoreType.DMA((len(pieces) * len(columns),))],
        ),
        out_shape=jax.ShapeDtypeStruct((size * rows, width), weight.dtype),
        compiler_params=pltpu.CompilerParams(vmem_limit_bytes=40 * 1024 * 1024),
        cost_estimate=pl.CostEstimate(
            flops=0, bytes_accessed=4 * size * rows * width, transcendentals=0
        ),
    )(jnp.stack(starts).astype(jnp.int32) // 16, *pieces)


def key_value_mixed():
    moves = [(0, 0, D)]
    for pair in range(PAIRS):
        target = D + 2 * LANES * pair
        moves += [(D + LANES * pair, target, LANES), (2 * D + LANES * pair, target + LANES, LANES)]
    return moves


def by_core(left, me, size):
    rows = left.shape[1] // size
    core = me & 1
    if rows % 128 == 0:
        return [
            jnp.concatenate(
                [lax.dynamic_slice_in_dim(left, (2 * i + which) * rows, rows, 1) for i in range(size // 2)], axis=1
            )
            for which in (1 - core, core)
        ]
    strips = [left[:, i * rows : (i + 1) * rows] for i in range(size)]
    even = jnp.concatenate(strips[0::2], axis=1)
    odd = jnp.concatenate(strips[1::2], axis=1)
    return jnp.where(core == 0, odd, even), jnp.where(core == 0, even, odd)


def group_step(part, bit, me):
    size_left, rows, columns = part.shape
    split = part.reshape(2, size_left // 2, rows, columns)
    side = (me >> bit) & 1
    send = lax.dynamic_index_in_dim(split, 1 - side, 0, keepdims=False)
    keep = lax.dynamic_index_in_dim(split, side, 0, keepdims=False)
    return send, keep


def group_sum(part, me, size, *until):
    for bit in range(bits_of(part.shape[0]), 0, -1):
        send, keep = group_step(part, bit, me)
        part = add_low(keep, swap(send, "grp", size, 1 << bit, *until))
    return part


def add_low(keep, got):
    return (keep.astype(F32) + got.astype(F32)).astype(BF16)


def rep_halves(part, rep):
    axis = part.ndim - 2
    half = part.shape[axis] // 2
    side = rep & 1
    send = lax.dynamic_slice_in_dim(part, (1 - side) * half, half, axis)
    keep = lax.dynamic_slice_in_dim(part, side * half, half, axis)
    return send, keep


def scatter_far(part, rep, reps, *until):
    count = reps // 2
    place = rep >> 1
    pieces = part.reshape(count, -1, part.shape[1])
    total = lax.dynamic_index_in_dim(pieces, place, 0, keepdims=False).astype(F32)
    for mask in range(1, count):
        send = lax.dynamic_index_in_dim(pieces, place ^ mask, 0, keepdims=False)
        total = total + swap(send, "rep", reps, mask << 1, *until).astype(F32)
    return total.astype(BF16)


def share_far(own, rep, reps, *until):
    count = reps // 2
    place = rep >> 1
    near = [own] + [swap(own, "rep", reps, mask << 1, *until) for mask in range(1, count)]
    ordered = []
    for i in range(count):
        value = near[i]
        for j in range(1, count):
            value = jnp.where(place == j, near[i ^ j], value)
        ordered.append(value)
    return jnp.concatenate(ordered, axis=0)


def as_rows(part):
    return jnp.concatenate([part[:, i : i + D] for i in range(0, part.shape[1], D)], axis=0)


def in_order(own, got, rep):
    side = rep & 1
    low, high = jnp.where(side == 0, own, got), jnp.where(side == 0, got, own)
    return jnp.concatenate([low, high], axis=0)


def total_vector(value, size, reps, pace, first):
    steps = [("grp", 0), ("rep", 0)] + [("grp", bit) for bit in range(1, bits_of(size))]
    steps += [("rep", bit) for bit in range(1, bits_of(reps))]
    for i, (axis, bit) in enumerate(steps):
        count = size if axis == "grp" else reps
        if (axis, bit) == ("rep", 1):
            value = value + first[0:1, :].astype(F32) * 0.0
        value = value + swap(value, axis, count, 1 << bit, pace[min(i, len(pace) - 1)])
    return value


def other_grad(left, right):
    return token_product(left, right).astype(BF16)


def core_grad(theirs, left, right, size):
    got = swap(theirs, "grp", size, 1).astype(F32)
    part = (token_product(left, right) + got).astype(BF16)
    return part.reshape(size // 2, -1, part.shape[1])


def dot_nt(left, right):
    return lax.dot_general(left, right, (((1,), (1,)), ((), ())), preferred_element_type=F32)


def dot_nn(left, right):
    return lax.dot_general(left, right, (((1,), (0,)), ((), ())), preferred_element_type=F32)


def one_head(pair, head):
    lane = lax.broadcasted_iota(jnp.int32, pair.shape, 1)
    inside = (lane < HD) if head == 0 else (lane >= HD)
    return jnp.where(inside, pair, jnp.zeros_like(pair))


def per_head(first, second, shape):
    lane = lax.broadcasted_iota(jnp.int32, shape, 1)
    return jnp.where(lane < HD, first, second)


def start_of(block, me, size, count):
    return pl.multiple_of(block_place(block, me, size) * count, count)


def query_mask(info, qseg, kseg, bias, tile, count):
    me = info[0]
    for q in range(count // tile):
        rows = pl.ds(q * tile, tile)

        def fill(block, _):
            columns = pl.ds(pl.multiple_of(block * count, count), count)
            q_pos = me * count + q * tile + lax.broadcasted_iota(jnp.int32, (tile, count), 0)
            k_pos = block * count + lax.broadcasted_iota(jnp.int32, (tile, count), 1)
            seen = (k_pos <= q_pos) & (qseg[rows, 0:1] == kseg[0:1, columns])
            bias[rows, columns] = jnp.where(seen, 0.0, NEG)
            return 0

        lax.fori_loop(info[1 + q], me + 1, fill, 0)


def attend_kernel(size, tile, skip, info, q_ref, k_ref, v_ref, qseg, kseg, *refs):
    out, out_low, lse, lse_row, bias = refs[skip:]
    count = q_ref.shape[0]
    me = info[0]

    @pl.when(pl.program_id(0) == 0)
    def _():
        query_mask(info, qseg, kseg, bias, tile, count)

    for q in range(count // tile):
        rows = pl.ds(q * tile, tile)
        queries = q_ref[rows, :] * jnp.asarray(SCALE, BF16)

        def step(block, carry):
            tops, sums, total = carry
            start = start_of(block, me, size, count)
            keys = k_ref[pl.ds(start, count), :]
            values = v_ref[pl.ds(start, count), :]
            add = bias[rows, pl.ds(pl.multiple_of(block * count, count), count)]
            new_tops, new_sums, shrinks = [], [], []
            gain = jnp.zeros((tile, LANES), F32)
            for head in range(2):
                scores = dot_nt(queries, one_head(keys, head)) + add
                top = jnp.maximum(tops[head], jnp.max(scores, axis=1, keepdims=True))
                weights = jnp.exp(scores - top)
                shrink = jnp.exp(tops[head] - top)
                new_tops.append(top)
                shrinks.append(shrink)
                new_sums.append(sums[head] * shrink + jnp.sum(weights, axis=1, keepdims=True))
                gain = gain + dot_nn(weights.astype(BF16), one_head(values, head))
            total = total * per_head(shrinks[0], shrinks[1], total.shape) + gain
            return (tuple(new_tops), tuple(new_sums), total)

        column = jnp.zeros((tile, 1), F32)
        tops, sums, total = lax.fori_loop(
            info[1 + q],
            me + 1,
            step,
            ((column + NEG, column + NEG), (column, column), jnp.zeros((tile, LANES), F32)),
        )
        shape = (tile, LANES)
        result = total / per_head(sums[0], sums[1], shape)
        log_total = per_head(tops[0] + jnp.log(sums[0]), tops[1] + jnp.log(sums[1]), shape)
        out[rows, :] = result
        out_low[rows, :] = result.astype(BF16)
        lse[rows, :] = log_total
        turned = log_total.T
        lse_row[0, :, rows] = jnp.zeros((8, tile), F32)
        lse_row[0, 0:1, rows] = turned[0:1, :]
        lse_row[0, 1:2, rows] = turned[HD : HD + 1, :]


def query_grad_kernel(size, tile, info, q_ref, k_ref, v_ref, dout, out, lse, qseg, kseg, dq, bias):
    count = q_ref.shape[0]
    me = info[0]

    @pl.when(pl.program_id(0) == 0)
    def _():
        query_mask(info, qseg, kseg, bias, tile, count)

    for q in range(count // tile):
        rows = pl.ds(q * tile, tile)
        queries = q_ref[rows, :] * jnp.asarray(SCALE, BF16)
        douts = dout[rows, :]
        both = douts.astype(F32) * out[rows, :]
        deltas = [jnp.sum(one_head(both, head), axis=1, keepdims=True) for head in range(2)]
        logs = [lse[rows, 0:1], lse[rows, HD : HD + 1]]

        def step(block, total):
            start = start_of(block, me, size, count)
            keys = k_ref[pl.ds(start, count), :]
            values = v_ref[pl.ds(start, count), :]
            add = bias[rows, pl.ds(pl.multiple_of(block * count, count), count)]
            for head in range(2):
                one_keys = one_head(keys, head)
                scores = dot_nt(queries, one_keys) + add
                probs = jnp.exp(scores - logs[head])
                prob_grad = dot_nt(douts, one_head(values, head))
                score_grad = (probs * (prob_grad - deltas[head])).astype(BF16)
                total = total + dot_nn(score_grad, one_keys)
            return total

        total = lax.fori_loop(info[1 + q], me + 1, step, jnp.zeros((tile, LANES), F32))
        dq[rows, :] = (total * SCALE).astype(BF16)


def key_grad_kernel(size, tile, info, k_ref, v_ref, q_ref, kseg, qseg, *refs):
    pieces, stat_pieces = refs[:size], refs[size : 2 * size]
    dkv, bias, dout, stats = refs[-4:]
    count = k_ref.shape[0]
    me = info[0]
    for i in range(size):
        dout[pl.ds(i * count, count), :] = pieces[i][...]
        stats[i] = stat_pieces[i][0]
    first = 1 + count // tile

    @pl.when(pl.program_id(0) == 0)
    def _():
        for k in range(count // tile):
            rows = pl.ds(k * tile, tile)

            def fill(block, _):
                columns = pl.ds(pl.multiple_of(block * count, count), count)
                k_pos = me * count + k * tile + lax.broadcasted_iota(jnp.int32, (tile, count), 0)
                q_pos = block * count + lax.broadcasted_iota(jnp.int32, (tile, count), 1)
                seen = (k_pos <= q_pos) & (kseg[rows, 0:1] == qseg[0:1, columns])
                bias[rows, columns] = jnp.where(seen, 0.0, NEG)
                return 0

            lax.fori_loop(me, info[first + k], fill, 0)

    for k in range(count // tile):
        rows = pl.ds(k * tile, tile)
        keys = k_ref[rows, :]
        values = v_ref[rows, :]

        def step(block, carry):
            key_total, value_total = carry
            place = block_place(block, me, size)
            start = pl.multiple_of(place * count, count)
            queries = q_ref[pl.ds(start, count), :] * jnp.asarray(SCALE, BF16)
            douts = dout[pl.ds(start, count), :]
            add = bias[rows, pl.ds(pl.multiple_of(block * count, count), count)]
            for head in range(2):
                one_queries = one_head(queries, head)
                one_douts = one_head(douts, head)
                scores = dot_nt(keys, one_queries) + add
                probs = jnp.exp(scores - stats[place, head : head + 1, :])
                prob_grad = dot_nt(values, one_douts)
                score_grad = probs * (prob_grad - stats[place, 2 + head : 3 + head, :])
                value_total = value_total + dot_nn(probs.astype(BF16), one_douts)
                key_total = key_total + dot_nn(score_grad.astype(BF16), one_queries)
            return (key_total, value_total)

        empty = jnp.zeros((tile, LANES), F32)
        key_total, value_total = lax.fori_loop(me, info[first + k], step, (empty, empty))
        dkv[rows, :LANES] = key_total.astype(BF16)
        dkv[rows, LANES:] = value_total.astype(BF16)


def strip(rows, first, stride=1):
    return pl.BlockSpec((rows, LANES), lambda p, info: (0, first + stride * p))


def whole(shape):
    return pl.BlockSpec(shape, lambda p, info: (0,) * len(shape))


def paired(count, first):
    return pl.BlockSpec((1, 8, count), lambda p, info: (first + p, 0, 0))


def call(body, in_specs, out_specs, out_shape, count, seq_len, products, pairs, mib=60, aliases=None, more_scratch=()):
    return pl.pallas_call(
        body,
        grid_spec=pltpu.PrefetchScalarGridSpec(
            num_scalar_prefetch=1,
            grid=(pairs,),
            in_specs=in_specs,
            out_specs=out_specs,
            scratch_shapes=[pltpu.VMEM((count, seq_len), F32), *more_scratch],
        ),
        out_shape=out_shape,
        input_output_aliases=aliases or {},
        compiler_params=pltpu.CompilerParams(vmem_limit_bytes=mib * 1024 * 1024),
        cost_estimate=pl.CostEstimate(
            flops=products * 2 * count * count * 2 * 256 * 2 * pairs,
            bytes_accessed=8 * 1024 * 1024,
            transcendentals=count * count * 4 * pairs,
        ),
    )


def key_value_strips(rows, first):
    return [strip(rows, PAIRS + 2 * first, 2), strip(rows, PAIRS + 2 * first + 1, 2)]


def attend(first, pairs, info, qkv_all, earlier, ready, seg_col, seg_row, count, seq_len, size, tile):
    out = jax.ShapeDtypeStruct((count, D), F32)
    return call(
        functools.partial(attend_kernel, size, tile, len(earlier) + len(ready)),
        [strip(count, first)]
        + key_value_strips(seq_len, first)
        + [whole((count, 128)), whole((1, seq_len))]
        + [pl.BlockSpec(memory_space=pl.ANY)] * (len(earlier) + len(ready)),
        [strip(count, first), strip(count, first), strip(count, first), paired(count, first)],
        [out, jax.ShapeDtypeStruct((count, D), BF16), out, jax.ShapeDtypeStruct((PAIRS, 8, count), F32)],
        count,
        seq_len,
        2,
        pairs,
        40,
        {6 + i: i for i in range(len(earlier))},
    )(info, qkv_all, qkv_all, qkv_all, seg_col, seg_row, *earlier, *ready)


def query_grads(first, pairs, info, qkv_all, dout, out, lse, seg_col, seg_row, count, seq_len, size, tile):
    return call(
        functools.partial(query_grad_kernel, size, tile),
        [strip(count, first)] + key_value_strips(seq_len, first)
        + [strip(count, first)] * 3
        + [whole((count, 128)), whole((1, seq_len))],
        strip(count, 0),
        jax.ShapeDtypeStruct((count, pairs * LANES), BF16),
        count,
        seq_len,
        3,
        pairs,
    )(info, qkv_all, qkv_all, qkv_all, dout, out, lse, seg_col, seg_row)


def key_grads(first, pairs, info, qkv_all, dout_all, stats, seg_col, seg_row, count, seq_len, size, tile):
    return call(
        functools.partial(key_grad_kernel, size, tile),
        key_value_strips(count, first)
        + [strip(seq_len, first)]
        + [whole((count, 128)), whole((1, seq_len))]
        + [strip(count, first)] * size
        + [paired(count, first)] * size,
        pl.BlockSpec((count, 2 * LANES), lambda p, info: (0, p)),
        jax.ShapeDtypeStruct((count, pairs * 2 * LANES), BF16),
        count,
        seq_len,
        4,
        pairs,
        more_scratch=[pltpu.VMEM((seq_len, LANES), BF16), pltpu.VMEM((size, 8, count), F32)],
    )(info, qkv_all, qkv_all, qkv_all, seg_col, seg_row, *dout_all, *stats)


def key_value_apart(columns):
    rows, width = columns.shape
    strips = [columns[:, i * LANES : (i + 1) * LANES] for i in range(width // LANES)]
    return strips[0::2], strips[1::2]


def per_device(
    reps,
    size,
    tokens,
    segment_ids,
    w_qkv,
    w_out,
    w_up,
    w_down,
    norm_gains,
    norm_shifts,
    proj_biases,
    up_bias,
    cotangent,
):
    count = tokens.shape[1]
    seq_len = segment_ids.shape[1]
    tile = min(512, count)
    me = lax.axis_index("grp")
    rep = lax.axis_index("rep")
    seg_row = segment_ids[0]
    first_row = me * count
    own_seg = lax.dynamic_slice_in_dim(seg_row, first_row, count, 0)
    seg_col = jnp.broadcast_to(own_seg[:, None], (count, 128))
    starts = own_seg[0::tile]
    ends = own_seg[tile - 1 :: tile]
    low = jnp.sum((seg_row[None, :] < starts[:, None]).astype(jnp.int32), axis=1) // count
    high = (jnp.sum((seg_row[None, :] <= ends[:, None]).astype(jnp.int32), axis=1) - 1) // count + 1
    info = jnp.concatenate([me[None].astype(jnp.int32), low, high])
    seg_row = seg_row[None]

    near_qkv = far_rows(w_qkv, rep, size, reps, True, (), (), ())
    first_far, last_far = near_qkv[1][2], near_qkv[-1][2]
    starts_qkv, pieces_qkv = both_cores(near_qkv, swap(w_qkv, "grp", size, 1), size, me, w_qkv.shape[0])
    other_out, other_up, other_down = [swap(weight, "grp", size, 1) for weight in (w_out, w_up, w_down)]
    qkv_full = place_rows(w_qkv, size, starts_qkv, pieces_qkv, key_value_mixed())

    source = tokens[0].astype(F32)
    normed = layer_norm(source, norm_gains[0], norm_shifts[0]).astype(BF16)
    normed_pieces = gather_pieces(after(normed, first_far), size, False, (last_far,), ())
    far_tokens = normed_pieces[1]
    normed_theirs, normed_mine = by_core(normed, me, size)
    normed_all = after(jnp.concatenate(normed_pieces, axis=0), normed_theirs, normed_mine)
    value_bias = proj_biases[1].reshape(PAIRS, LANES)
    bias = jnp.stack([jnp.zeros_like(value_bias), value_bias], axis=1).reshape(-1)
    shift = jnp.concatenate([proj_biases[0], bias])
    qkv_all = (add_rows(normed_all, qkv_full) + shift).astype(BF16)
    heads = (info, qkv_all)
    shapes = (seg_col, seg_row, count, seq_len, size, tile)
    part = PAIRS // 2
    earlier = attend(0, part, *heads, (), (other_out, other_up, other_down), *shapes)
    near_up = far_rows(w_up, rep, size, reps, True, (far_tokens,), earlier, ())
    near_out = far_rows(w_out, rep, size, reps, False, (far_tokens,), earlier, ())
    starts_out, pieces_out = both_cores(near_out, other_out, size, me, w_out.shape[0])
    starts_up, pieces_up = both_cores(near_up, other_up, size, me, w_up.shape[0])
    ready = pieces_out[2:] + pieces_up[2:4]
    attended_f, attended, lse, lse_row = attend(part, part, *heads, earlier, ready, *shapes)
    pieces_out[0], pieces_up[0] = after(pieces_out[0], attended), after(pieces_up[0], attended)
    near_down = far_rows(w_down, rep, size, reps, True, (near_up[1][2],), (attended,), ())
    out_full = place_rows(w_out, size, starts_out, pieces_out)
    middle = source + add_rows(attended, out_full) + proj_biases[2]
    up_full = place_rows(w_up, size, starts_up, pieces_up)
    second = layer_norm(middle, norm_gains[1], norm_shifts[1]).astype(BF16)
    hidden_pre = add_rows(second, up_full) + up_bias
    hidden = jax.nn.gelu(hidden_pre).astype(BF16)
    upstream = cotangent[0]
    upstream_f = upstream.astype(F32)
    hidden_theirs, hidden_mine = by_core(hidden, me, size)
    down_theirs = other_grad(hidden_theirs, upstream)
    near_down = [(near, first, after(piece, hidden)) for near, first, piece in near_down]
    starts_down, pieces_down = both_cores(near_down, other_down, size, me, w_down.shape[0], (down_theirs,))
    down_full = place_rows(w_down, size, starts_down, pieces_down)
    hidden_grad = back_rows(after(upstream, down_theirs), down_full)
    _, gelu_pull = jax.vjp(jax.nn.gelu, hidden_pre)
    pre_grad = gelu_pull(hidden_grad)[0].astype(BF16)
    second_theirs, second_mine = by_core(second, me, size)
    up_theirs = other_grad(second_theirs, pre_grad)
    down_part = core_grad(down_theirs, after(hidden_mine, up_theirs), upstream, size)
    down_send, down_keep = group_step(down_part, bits_of(size) - 1, me)

    up_part = core_grad(up_theirs, second_mine, after(pre_grad, down_send), size)
    up_send, up_keep = rep_halves(up_part, rep)

    second_grad = back_rows(after(pre_grad, up_send), up_full)
    _, second_pull = jax.vjp(layer_norm, middle, norm_gains[1], norm_shifts[1])
    middle_part, gain_second, shift_second = second_pull(second_grad)
    middle_grad = upstream_f + middle_part
    branch_grad = middle_grad.astype(BF16)
    dout = back_rows(branch_grad, out_full).astype(BF16)
    row = lax.broadcasted_iota(jnp.int32, (8 * PAIRS, D), 0)
    minor = row % 8 - 2
    lane_head = lax.broadcasted_iota(jnp.int32, (8 * PAIRS, D), 1) // HD
    picks = ((row // 8 * 2 + minor == lane_head) & (minor >= 0) & (minor < 2)).astype(F32)
    delta_row = jnp.einsum(
        "ed,td->et", picks, dout.astype(F32) * attended_f, precision=lax.Precision.HIGHEST
    ).reshape(PAIRS, 8, count)

    attended_theirs, attended_mine = by_core(after(attended, dout), me, size)
    out_theirs = other_grad(attended_theirs, after(branch_grad, dout))
    queries_one = query_grads(0, part, *heads, after(dout, up_send, out_theirs, delta_row), attended_f, lse, *shapes)

    out_part = core_grad(out_theirs, attended_mine, after(branch_grad, queries_one), size)
    down_part = add_low(down_keep, swap(down_send, "grp", size, size // 2, queries_one))
    down_send, down_keep = rep_halves(group_sum(down_part, me, size)[0], rep)
    up_part = add_low(up_keep, swap(up_send, "rep", reps, 1, queries_one))
    up_send, up_keep = group_step(up_part, bits_of(size) - 1, me)
    queries_two = query_grads(part, part, *heads, after(dout, up_send, down_send, out_part), attended_f, lse, *shapes)
    down_part = add_low(down_keep, swap(down_send, "rep", reps, 1, queries_two))
    up_part = add_low(up_keep, swap(up_send, "grp", size, size // 2, queries_two))
    up_part = group_sum(up_part, me, size)[0]
    both_part = jnp.concatenate([down_part, as_rows(up_part)], axis=0)
    stats = gather_pieces(lse_row + delta_row, size, True, (queries_two,), ())
    dout_all = gather_pieces(dout, size, True, (queries_two,), ())

    both_queries = jnp.concatenate([queries_one, queries_two], axis=1)
    query_theirs = other_grad(normed_theirs, after(both_queries, both_part))
    mixed_one = key_grads(0, part, *heads, [after(dout_all[0], query_theirs, both_part)] + dout_all[1:], stats, *shapes)

    query_part = core_grad(query_theirs, normed_mine, after(both_queries, mixed_one), size)
    pair_part = jnp.concatenate([query_part, out_part], axis=1)
    pair_send, pair_keep = group_step(pair_part, bits_of(size) - 1, me)
    one_theirs = other_grad(normed_theirs, mixed_one)
    both_part = scatter_far(both_part, rep, reps, mixed_one)
    one_part = core_grad(one_theirs, normed_mine, mixed_one, size)
    one_send, one_keep = group_step(one_part, bits_of(size) - 1, me)
    mixed_two = key_grads(
        part, part, *heads, [after(dout_all[0], one_send, pair_send, both_part)] + dout_all[1:], stats, *shapes
    )

    two_theirs = other_grad(normed_theirs, mixed_two)
    two_part = core_grad(two_theirs, normed_mine, mixed_two, size)
    two_send, two_keep = group_step(two_part, bits_of(size) - 1, me)
    one_part = add_low(after(one_keep, two_send), swap(one_send, "grp", size, size // 2, mixed_two))
    pair_part = add_low(after(pair_keep, two_theirs), swap(pair_send, "grp", size, size // 2, mixed_two))
    pair_send, pair_keep = rep_halves(group_sum(pair_part, me, size)[0], rep)
    both_every = share_far(both_part, rep, reps, mixed_two)

    joined_grad = jnp.concatenate([both_queries, mixed_one, mixed_two], axis=1)
    normed_grad = back_rows(after(joined_grad, two_send, pair_send), qkv_full)
    _, first_pull = jax.vjp(layer_norm, source, norm_gains[0], norm_shifts[0])
    source_part, gain_first, shift_first = first_pull(normed_grad)
    input_grad = middle_grad + source_part
    joined_sum = jnp.sum(joined_grad.astype(F32), axis=0, keepdims=True)
    value_sum = joined_sum[:, D:].reshape(PAIRS, 2, LANES)[:, 1].reshape(1, D)
    pre_sum = jnp.sum(pre_grad.astype(F32), axis=0, keepdims=True)
    vectors = jnp.concatenate(
        [
            gain_first[None],
            gain_second[None],
            shift_first[None],
            shift_second[None],
            joined_sum[:, :D],
            value_sum,
            jnp.sum(branch_grad.astype(F32), axis=0, keepdims=True),
            jnp.sum(upstream_f, axis=0, keepdims=True),
            *[pre_sum[:, i : i + D] for i in range(0, FF, D)],
        ],
        axis=0,
    )

    two_part = add_low(two_keep, swap(two_send, "grp", size, size // 2, vectors))
    mixed_part = group_sum(jnp.concatenate([one_part, two_part], axis=1), me, size)[0]
    mixed_send, mixed_keep = rep_halves(mixed_part, rep)
    pair_part = add_low(pair_keep, swap(pair_send, "rep", reps, 1, mixed_send))
    nothing = mixed_send[0:1, :].astype(F32) * 0.0
    block_out = (middle + add_rows(hidden, down_full) + (proj_biases[3] + nothing)).astype(BF16)
    pace = [mixed_send, mixed_send]
    mixed_part = add_low(mixed_keep, swap(mixed_send, "rep", reps, 1, block_out))

    both_got = swap(after(both_every, block_out), "rep", reps, 1)
    pair_part = scatter_far(after(pair_part, mixed_part), rep, reps)
    mixed_part = scatter_far(mixed_part, rep, reps)
    pair_every = share_far(pair_part, rep, reps, mixed_part)
    mixed_every = share_far(mixed_part, rep, reps, pair_every)
    mixed_got = swap(mixed_every, "rep", reps, 1)
    pace += [mixed_part, mixed_every, mixed_got]
    pair_got = swap(pair_every, "rep", reps, 1, mixed_every)
    vectors = total_vector(vectors, size, reps, pace, both_got)

    rows = w_qkv.shape[0]
    tall = w_down.shape[0] // 2
    grad_down = in_order(both_every[:tall], both_got[:tall], rep)
    wide = [
        in_order(both_every[i : i + rows // 2], both_got[i : i + rows // 2], rep)
        for i in range(tall, both_every.shape[0], rows // 2)
    ]
    grad_up = jnp.concatenate(wide, axis=1)
    pair_grad = in_order(pair_every, pair_got, rep).astype(F32)
    mixed_grad = in_order(mixed_every, mixed_got, rep).astype(F32)
    one_keys, one_values = key_value_apart(mixed_grad[:rows])
    two_keys, two_values = key_value_apart(mixed_grad[rows:])
    grad_qkv = jnp.concatenate([pair_grad[:rows]] + one_keys + two_keys + one_values + two_values, axis=1)
    grad_out = pair_grad[rows:]
    return (
        block_out[None],
        input_grad[None],
        grad_qkv,
        grad_out,
        grad_up.astype(F32),
        grad_down.astype(F32),
        vectors[:2],
        vectors[2:4],
        vectors[4:8],
        vectors[8:].reshape(-1),
    )


def solution(mesh):
    return jax.shard_map(
        functools.partial(per_device, mesh.shape["rep"], mesh.shape["grp"]),
        mesh=mesh,
        in_specs=(
            P("rep", "grp", None),
            P("rep", None),
            P("grp", None),
            P("grp", None),
            P("grp", None),
            P("grp", None),
            P(),
            P(),
            P(),
            P(),
            P("rep", "grp", None),
        ),
        out_specs=(
            P("rep", "grp", None),
            P("rep", "grp", None),
            P("grp", None),
            P("grp", None),
            P("grp", None),
            P("grp", None),
            P(),
            P(),
            P(),
            P(),
        ),
        check_vma=False,
    )
```

profile of v0, /device:TPU:0, one launch (start us, length us, event | category | flops | bytes accessed | tf_op | source)
XLA Modules:
  0.0 354.4 jit_solution(10004856924522256924)
XLA Ops:
  1.8 3.0 collective-permute-start
  7.9 7.2 %collective-permute-done.refs_2_ = bf16[96,2304]{1,0:T(8,128)(2,1)S(1)} collective-permute-done((bf16[96,2304]{1,0:T(8,128)(2,1)S(1)}, bf16[96,2304]{1,0:T(8,128)(2,1)S(1)}, u32[]{:S(2)}, u32[]{:S(2)}) %collective-permute-start) | collective-permute-done | bytes 442400 | tf_op jit(solution)/shard_map/ppermute | solution.py:46
  15.0 1.7 collective-permute-start.1
  17.4 1.9 fusion.89
  27.8 8.2 %collective-permute-done.2.refs_4_ = bf16[96,2304]{1,0:T(8,128)(2,1)S(1)} collective-permute-done((bf16[96,2304]{1,0:T(8,128)(2,1)S(1)}, bf16[96,2304]{1,0:T(8,128)(2,1)S(1)}, u32[]{:S(2)}, u32[]{:S(2)}) %collective-permute-start.2) | collective-permute-done | bytes 442400 | tf_op jit(solution)/shard_map/ppermute | solution.py:46
  36.8 2.1 collective-permute-done.6.refs_3_
  39.7 2.1 shard_map.186
  42.1 1.7 collective-permute-start.11
  45.4 9.6 %add_convert_fusion.q_ref.k_ref.v_ref = bf16[2048,2304]{1,0:T(8,128)(2,1)} fusion(bf16[2048,768]{1,0:T(8,128)(2,1)S(1)} %pad_maximum_fusion, bf16[768,2304]{1,0:T(8,128)(2,1)S(1)} %shard_map.186, f32[2304]{0:T(1024)S(1)} %pad_maximum_fusion.22), kind=kOutput, calls=%fused_computation | convolution fusion | flops 7257194496 | bytes 16131072 | tf_op jit(solution)/shard_map/dot_general | solution.py:30
  55.2 7.6 %shard_map.187 = (f32[512,768]{1,0:T(8,128)S(1)}, bf16[512,768]{1,0:T(8,128)(2,1)S(1)}, f32[512,768]{1,0:T(8,128)S(1)}, f32[6,8,512]{2,1,0:T(8,128)S(1)}) custom-call(s32[3]{0:T(128)S(1)} %pad_add_fusion.info, bf16[2048,2304]{1,0:T(8,128)(2,1)} %add_convert_fusion.q_ref.k_ref.v_ref, bf16[2048,2304]{1,0:T(8,128)(2,1)} %add_convert_fusion.q_ref.k_ref.v_ref, ...), custom_call_target="tpu_custom_call" | custom-call | flops 3221225472 | bytes 8388608 | tf_op jit(solution)/shard_map/pallas_call | solution.py:466
  63.8 3.7 %collective-permute-start.14 = (bf16[96,3072]{1,0:T(8,128)(2,1)}, bf16[96,3072]{1,0:T(8,128)(2,1)}, u32[]{:S(2)}, u32[]{:S(2)}) collective-permute-start(bf16[96,3072]{1,0:T(8,128)(2,1)} %collective-permute-done.13.refs_6_.refs_2_), channel_id=1, source_target_pairs={{0,1},{1,0},{2,3},{3,2},{4,5},{5,4},{6,7},{7,6},{8,9},{9,8},{10,11... | collective-permute-start | bytes 1769480 | tf_op jit(solution)/shard_map/ppermute | solution.py:46
  69.9 1.8 collective-permute-start.15
  71.7 7.3 %shard_map.188 = (f32[512,768]{1,0:T(8,128)S(1)}, bf16[512,768]{1,0:T(8,128)(2,1)S(1)}, f32[512,768]{1,0:T(8,128)S(1)}, f32[6,8,512]{2,1,0:T(8,128)S(1)}) custom-call(s32[3]{0:T(128)S(1)} %pad_add_fusion.info, bf16[2048,2304]{1,0:T(8,128)(2,1)} %add_convert_fusion.q_ref.k_ref.v_ref, ...), custom_call_target="tpu_custom_call", output_to_operand_aliasing={{0}: (6, {}), {1}: (7, {}), {2}: (8, {}), {3}: (9, {})} | custom-call | flops 3221225472 | bytes 8388608 | tf_op jit(solution)/shard_map/pallas_call | solution.py:466
  79.1 5.4 %collective-permute-done.17.refs_2_ = bf16[384,768]{1,0:T(8,128)(2,1)S(1)} collective-permute-done((bf16[384,768]{1,0:T(8,128)(2,1)S(1)}, bf16[384,768]{1,0:T(8,128)(2,1)S(1)}, u32[]{:S(2)}, u32[]{:S(2)}) %collective-permute-start.17) | collective-permute-done | bytes 589856 | tf_op jit(solution)/shard_map/ppermute | solution.py:46
  86.0 1.6 shard_map.189
  90.9 2.3 shard_map.190
  93.2 4.0 %multiply_convert_fusion = (bf16[512,3072]{1,0:T(8,128)(2,1)S(1)}, f32[512,3072]{1,0:T(8,128)S(1)}) fusion(f32[3072]{0:T(1024)S(1)} %copy-done.90, bf16[512,768]{1,0:T(8,128)(2,1)S(1)} %add_convert_fusion.5, bf16[768,3072]{1,0:T(8,128)(2,1)S(1)} %shard_map.190), kind=kOutput, calls=%fused_computation.11 | convolution fusion | flops 2431647744 | bytes 14954496 | tf_op jit(solution)/shard_map/dot_general | solution.py:30
  97.3 2.2 collective-permute-done.19.refs_4_
  101.9 2.8 convolution_convert_fusion.1
  104.8 1.6 shard_map.191
  106.4 7.1 %convert_reduce_fusion = (f32[3072]{0:T(1024)}, bf16[512,3072]{1,0:T(8,128)(2,1)S(1)}) fusion(f32[512,3072]{1,0:T(8,128)S(1)} %get-tuple-element.257, f32[3072]{0:T(1024)S(1)} %copy-done.90, bf16[512,768]{1,0:T(8,128)(2,1)S(1)} %bitcast.190, bf16[3072,768]{1,0:T(8,128)(2,1)S(1)} %shard_map.191), kind=kOutput, calls=%fused_computation.10 | convolution fusion | flops 2452091904 | bytes 14966784 | tf_op jit(solution)/shard_map/te,ce->tc/dot_general | solution.py:34
  113.5 3.0 convolution_convert_fusion
  119.0 3.2 add_convert_fusion.2
  124.1 4.1 %add_convert_fusion.1 = bf16[384,3072]{1,0:T(8,128)(2,1)S(1)} fusion(bf16[384,3072]{1,0:T(8,128)(2,1)} %collective-permute-done.22, bf16[512,3072]{1,0:T(8,128)(2,1)S(1)} %copy-done.37, pred[]{:T(512)S(6)} %eq.14, bf16[512,192]{1,0:T(8,128)(2,1)S(1)} %copy-done.52, bf16[512,192]{1,0:T(8,128)(2,1)S(1)} %copy-done.54, bf16[512,192]{1,0:T(8,128)(2,1)S(1)} %copy-done.56, ...), kind=kOutput, calls=%fused_computation.13 | convolution fusion | flops 1213267968 | bytes 8650753 | tf_op jit(solution)/shard_map/tc,te->ce/dot_general | solution.py:38
  130.7 3.0 multiply_reduce_fusion
  142.6 7.8 %shard_map.192 = bf16[512,384]{1,0:T(8,128)(2,1)} custom-call(s32[3]{0:T(128)} %copy-done.25, bf16[2048,2304]{1,0:T(8,128)(2,1)} %add_convert_fusion.q_ref.k_ref.v_ref, bf16[2048,2304]{1,0:T(8,128)(2,1)} %add_convert_fusion.q_ref.k_ref.v_ref, bf16[2048,2304]{1,0:T(8,128)(2,1)} %add_convert_fusion.q_ref.k_ref.v_ref, bf16[512,768]{1,0:T(8,128)(2,1)} %copy-done.29, ...), custom_call_target="tpu_custom_call" | custom-call | flops 4831838208 | bytes 8388608 | tf_op jit(solution)/shard_map/pallas_call | solution.py:484
  154.1 2.0 fusion.7
  157.5 2.7 add_convert_fusion.8
  160.2 5.9 %collective-permute-done.23 = bf16[2,96,3072]{2,1,0:T(8,128)(2,1)} collective-permute-done((bf16[2,96,3072]{2,1,0:T(8,128)(2,1)}, bf16[2,96,3072]{2,1,0:T(8,128)(2,1)}, u32[]{:S(2)}, u32[]{:S(2)}) %collective-permute-start.23) | collective-permute-done | bytes 1179680 | tf_op jit(solution)/shard_map/ppermute | solution.py:46
  166.2 1.7 add_convert_fusion.3
  168.7 1.9 collective-permute-start.27
  170.6 7.8 %shard_map.193 = bf16[512,384]{1,0:T(8,128)(2,1)} custom-call(s32[3]{0:T(128)} %copy-done.25, bf16[2048,2304]{1,0:T(8,128)(2,1)} %add_convert_fusion.q_ref.k_ref.v_ref, bf16[2048,2304]{1,0:T(8,128)(2,1)} %add_convert_fusion.q_ref.k_ref.v_ref, bf16[2048,2304]{1,0:T(8,128)(2,1)} %add_convert_fusion.q_ref.k_ref.v_ref, bf16[512,768]{1,0:T(8,128)(2,1)} %copy-done.29, ...), custom_call_target="tpu_custom_call" | custom-call | flops 4831838208 | bytes 8388608 | tf_op jit(solution)/shard_map/pallas_call | solution.py:484
  178.4 3.5 %collective-permute-start.32 = (f32[6,8,512]{2,1,0:T(8,128)}, f32[6,8,512]{2,1,0:T(8,128)S(1)}, u32[]{:S(2)}, u32[]{:S(2)}) collective-permute-start(f32[6,8,512]{2,1,0:T(8,128)} %add.394.refs_4_), channel_id=1, source_target_pairs={{0,1},{1,0},{2,3},{3,2},{4,5},{5,4},{6,7},{7,6},{8,9},{9,8},{10,11... | collective-permute-start | bytes 294920 | tf_op jit(solution)/shard_map/ppermute | solution.py:46
  188.2 1.6 collective-permute-start.36
  189.9 18.0 %collective-permute-start.37 = (bf16[192,768]{1,0:T(8,128)(2,1)S(1)}, bf16[192,768]{1,0:T(8,128)(2,1)S(1)}, u32[]{:S(2)}, u32[]{:S(2)}) collective-permute-start(bf16[192,768]{1,0:T(8,128)(2,1)S(1)} %get-tuple-element.207), channel_id=1, source_target_pairs={{0,16},{4,20},{8,24},{12,28},{16,0},{20,4},{24,8},{28,12},{1,17},{... | collective-permute-start | bytes 884744 | tf_op jit(solution)/shard_map/ppermute | solution.py:46
  207.9 2.0 collective-permute-start.38
  209.9 12.3 %shard_map.194 = bf16[512,768]{1,0:T(8,128)(2,1)} custom-call(s32[3]{0:T(128)} %copy-done.25, bf16[2048,2304]{1,0:T(8,128)(2,1)} %add_convert_fusion.q_ref.k_ref.v_ref, bf16[2048,2304]{1,0:T(8,128)(2,1)} %add_convert_fusion.q_ref.k_ref.v_ref, bf16[2048,2304]{1,0:T(8,128)(2,1)} %add_convert_fusion.q_ref.k_ref.v_ref, s32[512,128]{1,0:T(8,128)} %copy-done.2, ...), custom_call_target="tpu_custom_call" | custom-call | flops 6442450944 | bytes 8388608 | tf_op jit(solution)/shard_map/pallas_call | solution.py:499
  222.2 1.7 convolution_convert_fusion.4
  224.0 5.0 %collective-permute-done.38 = bf16[192,768]{1,0:T(8,128)(2,1)S(1)} collective-permute-done((bf16[192,768]{1,0:T(8,128)(2,1)S(1)}, bf16[192,768]{1,0:T(8,128)(2,1)S(1)}, u32[]{:S(2)}, u32[]{:S(2)}) %collective-permute-start.38) | collective-permute-done | bytes 294944 | tf_op jit(solution)/shard_map/ppermute | solution.py:46
  230.2 5.9 %collective-permute-start.59 = (bf16[192,768]{1,0:T(8,128)(2,1)S(1)}, bf16[192,768]{1,0:T(8,128)(2,1)S(1)}, u32[]{:S(2)}, u32[]{:S(2)}) collective-permute-start(bf16[192,768]{1,0:T(8,128)(2,1)S(1)} %fusion.45), channel_id=1, source_target_pairs={{0,8},{4,12},{8,0},{12,4},{16,24},{20,28},{24,16},{28,20},{1,9},{5... | collective-permute-start | bytes 884744 | tf_op jit(solution)/shard_map/ppermute | solution.py:46
  236.1 2.0 collective-permute-start.61
  244.6 12.3 %shard_map.195 = bf16[512,768]{1,0:T(8,128)(2,1)} custom-call(s32[3]{0:T(128)} %copy-done.25, bf16[2048,2304]{1,0:T(8,128)(2,1)} %add_convert_fusion.q_ref.k_ref.v_ref, bf16[2048,2304]{1,0:T(8,128)(2,1)} %add_convert_fusion.q_ref.k_ref.v_ref, bf16[2048,2304]{1,0:T(8,128)(2,1)} %add_convert_fusion.q_ref.k_ref.v_ref, s32[512,128]{1,0:T(8,128)} %copy-done.2, ...), custom_call_target="tpu_custom_call" | custom-call | flops 6442450944 | bytes 8388608 | tf_op jit(solution)/shard_map/pallas_call | solution.py:499
  256.9 1.6 convolution_convert_fusion.3
  265.5 6.7 %collective-permute-start.43 = (bf16[192,768]{1,0:T(8,128)(2,1)}, bf16[192,768]{1,0:T(8,128)(2,1)}, u32[]{:S(2)}, u32[]{:S(2)}) collective-permute-start(bf16[192,768]{1,0:T(8,128)(2,1)} %dynamic-slice_bitcast_fusion.2), channel_id=1, source_target_pairs={{0,4},{4,0},{8,12},{12,8},{16,20},{20,16},{24,28},{28,24},{1,5},{5... | collective-permute-start | bytes 884744 | tf_op jit(solution)/shard_map/ppermute | solution.py:46
  274.8 2.1 fusion.20
  278.6 1.9 add_bitcast_fusion
  284.9 1.8 collective-permute-start.64
  286.7 6.8 %add_convert_fusion.4 = bf16[512,768]{1,0:T(8,128)(2,1)} fusion(f32[512,768]{1,0:T(8,128)S(1)} %copy-done.33, bf16[512,3072]{1,0:T(8,128)(2,1)} %copy-done.42, bf16[3072,768]{1,0:T(8,128)(2,1)} %copy-done.7, f32[768]{0:T(1024)S(1)} %fusion.99), kind=kOutput, calls=%fused_computation.47 | convolution fusion | flops 2417098752 | bytes 10226688 | tf_op jit(solution)/shard_map/dot_general | solution.py:30
  296.3 4.3 %collective-permute-start.45 = (bf16[48,768]{1,0:T(8,128)(2,1)S(1)}, bf16[48,768]{1,0:T(8,128)(2,1)S(1)}, u32[]{:S(2)}, u32[]{:S(2)}) collective-permute-start(bf16[48,768]{1,0:T(8,128)(2,1)S(1)} %get-tuple-element.241), channel_id=1, source_target_pairs={{0,8},{4,12},{8,0},{12,4},{16,24},{20,28},{24,16},{28,20},{1,9},{5... | collective-permute-start | bytes 221192 | tf_op jit(solution)/shard_map/ppermute | solution.py:46
  300.7 5.7 %collective-permute-start.46 = (bf16[48,768]{1,0:T(8,128)(2,1)S(1)}, bf16[48,768]{1,0:T(8,128)(2,1)S(1)}, u32[]{:S(2)}, u32[]{:S(2)}) collective-permute-start(bf16[48,768]{1,0:T(8,128)(2,1)S(1)} %get-tuple-element.243), channel_id=1, source_target_pairs={{0,16},{4,20},{8,24},{12,28},{16,0},{20,4},{24,8},{28,12},{1,17},{... | collective-permute-start | bytes 221192 | tf_op jit(solution)/shard_map/ppermute | solution.py:46
  309.7 2.7 collective-permute-start.50
  313.3 2.6 collective-permute-start.51
  318.1 1.9 collective-permute-done.51
  320.0 2.8 collective-permute-start.48
  322.9 2.9 collective-permute-start.57
  325.8 4.0 %collective-permute-start.55 = (bf16[48,768]{1,0:T(8,128)(2,1)S(1)}, bf16[48,768]{1,0:T(8,128)(2,1)S(1)}, u32[]{:S(2)}, u32[]{:S(2)}) collective-permute-start(bf16[48,768]{1,0:T(8,128)(2,1)S(1)} %fusion.65), channel_id=1, source_target_pairs={{0,24},{4,28},{8,16},{12,20},{16,8},{20,12},{24,0},{28,4},{1,25},{... | collective-permute-start | bytes 221192 | tf_op jit(solution)/shard_map/ppermute | solution.py:46
  329.8 2.3 collective-permute-start.54
  332.5 2.0 collective-permute-start.58
  334.5 4.4 %collective-permute-done.54 = bf16[192,768]{1,0:T(8,128)(2,1)S(1)} collective-permute-done((bf16[192,768]{1,0:T(8,128)(2,1)S(1)}, bf16[192,768]{1,0:T(8,128)(2,1)S(1)}, u32[]{:S(2)}, u32[]{:S(2)}) %collective-permute-start.54) | collective-permute-done | bytes 294944 | tf_op jit(solution)/shard_map/ppermute | solution.py:46
  340.0 2.1 collective-permute-done.58
  343.7 1.7 maximum_convert_fusion
  346.7 2.4 collective-permute-start.67
  349.1 1.6 maximum_convert_fusion.1
  350.7 1.6 collective-permute-done.67
  (420 shorter events, 90.0 us)
Async XLA Ops:
  1.8 13.2 %collective-permute-start = (bf16[96,2304]{1,0:T(8,128)(2,1)S(1)}, bf16[96,2304]{1,0:T(8,128)(2,1)S(1)}, u32[]{:S(2)}, u32[]{:S(2)}) collective-permute-start(bf16[96,2304]{1,0:T(8,128)(2,1)S(1)} %constant_dynamic-slice_fusion.10), channel_id=1, source_target_pairs={{0,2},{1,3},{2,0},{3,1},{4,6},{5,7},{6,4},{7,5},{8,10},{9,11},{10,... | collective-permute-start | bytes 1327112 | tf_op jit(solution)/shard_map/ppermute | solution.py:46
  15.0 20.9 %collective-permute-start.1 = (bf16[512,768]{1,0:T(8,128)(2,1)}, bf16[512,768]{1,0:T(8,128)(2,1)}, u32[]{:S(2)}, u32[]{:S(2)}) collective-permute-start(bf16[512,768]{1,0:T(8,128)(2,1)} %fusion.17), channel_id=1, source_target_pairs={{0,2},{1,3},{2,0},{3,1},{4,6},{5,7},{6,4},{7,5},{8,10},{9,11},{10,... | collective-permute-start | bytes 2359304 | tf_op jit(solution)/shard_map/ppermute | solution.py:59
  16.8 22.2 %collective-permute-start.5 = (bf16[192,2304]{1,0:T(8,128)(2,1)S(1)}, bf16[192,2304]{1,0:T(8,128)(2,1)S(1)}, u32[]{:S(2)}, u32[]{:S(2)}) collective-permute-start(bf16[192,2304]{1,0:T(8,128)(2,1)S(1)} %copy-done.19), channel_id=1, source_target_pairs={{0,1},{1,0},{2,3},{3,2},{4,5},{5,4},{6,7},{7,6},{8,9},{9,8},{10,11... | collective-permute-start | bytes 2654216 | tf_op jit(solution)/shard_map/ppermute | solution.py:46
  23.4 12.6 %collective-permute-start.2 = (bf16[96,2304]{1,0:T(8,128)(2,1)S(1)}, bf16[96,2304]{1,0:T(8,128)(2,1)S(1)}, u32[]{:S(2)}, u32[]{:S(2)}) collective-permute-start(bf16[96,2304]{1,0:T(8,128)(2,1)S(1)} %collective-permute-done.refs_2_), channel_id=1, source_target_pairs={{0,4},{4,0},{8,12},{12,8},{16,20},{20,16},{24,28},{28,24},{1,5},{5... | collective-permute-start | bytes 1327112 | tf_op jit(solution)/shard_map/ppermute | solution.py:46
  27.6 14.2 %collective-permute-start.3 = (bf16[512,768]{1,0:T(8,128)(2,1)}, bf16[512,768]{1,0:T(8,128)(2,1)S(1)}, u32[]{:S(2)}, u32[]{:S(2)}) collective-permute-start(bf16[512,768]{1,0:T(8,128)(2,1)} %fusion.17), channel_id=1, source_target_pairs={{0,1},{1,0},{2,3},{3,2},{4,5},{5,4},{6,7},{7,6},{8,9},{9,8},{10,11... | collective-permute-start | bytes 2359304 | tf_op jit(solution)/shard_map/ppermute | solution.py:46
  36.0 6.2 %collective-permute-start.4 = (bf16[512,768]{1,0:T(8,128)(2,1)}, bf16[512,768]{1,0:T(8,128)(2,1)S(1)}, u32[]{:S(2)}, u32[]{:S(2)}) collective-permute-start(bf16[512,768]{1,0:T(8,128)(2,1)} %collective-permute-done.1), channel_id=1, source_target_pairs={{0,1},{1,0},{2,3},{3,2},{4,5},{5,4},{6,7},{7,6},{8,9},{9,8},{10,11... | collective-permute-start | bytes 2359304 | tf_op jit(solution)/shard_map/ppermute | solution.py:46
  38.9 16.2 %collective-permute-start.9 = (bf16[192,3072]{1,0:T(8,128)(2,1)S(1)}, bf16[192,3072]{1,0:T(8,128)(2,1)S(1)}, u32[]{:S(2)}, u32[]{:S(2)}) collective-permute-start(bf16[192,3072]{1,0:T(8,128)(2,1)S(1)} %copy-done.15), channel_id=1, source_target_pairs={{0,1},{1,0},{2,3},{3,2},{4,5},{5,4},{6,7},{7,6},{8,9},{9,8},{10,11... | collective-permute-start | bytes 3538952 | tf_op jit(solution)/shard_map/ppermute | solution.py:46
  39.0 16.0 %collective-permute-start.8 = (bf16[192,768]{1,0:T(8,128)(2,1)}, bf16[192,768]{1,0:T(8,128)(2,1)S(1)}, u32[]{:S(2)}, u32[]{:S(2)}) collective-permute-start(bf16[192,768]{1,0:T(8,128)(2,1)} %refs_0_.2), channel_id=1, source_target_pairs={{0,1},{1,0},{2,3},{3,2},{4,5},{5,4},{6,7},{7,6},{8,9},{9,8},{10,11... | collective-permute-start | bytes 884744 | tf_op jit(solution)/shard_map/ppermute | solution.py:46
  39.5 15.5 %collective-permute-start.10 = (bf16[768,768]{1,0:T(8,128)(2,1)S(1)}, bf16[768,768]{1,0:T(8,128)(2,1)S(1)}, u32[]{:S(2)}, u32[]{:S(2)}) collective-permute-start(bf16[768,768]{1,0:T(8,128)(2,1)S(1)} %copy-done.17), channel_id=1, source_target_pairs={{0,1},{1,0},{2,3},{3,2},{4,5},{5,4},{6,7},{7,6},{8,9},{9,8},{10,11... | collective-permute-start | bytes 3538952 | tf_op jit(solution)/shard_map/ppermute | solution.py:46
  41.8 22.0 %collective-permute-start.13 = (bf16[96,3072]{1,0:T(8,128)(2,1)S(1)}, bf16[96,3072]{1,0:T(8,128)(2,1)}, u32[]{:S(2)}, u32[]{:S(2)}) collective-permute-start(bf16[96,3072]{1,0:T(8,128)(2,1)S(1)} %constant_dynamic-slice_fusion.9), channel_id=1, source_target_pairs={{0,2},{1,3},{2,0},{3,1},{4,6},{5,7},{6,4},{7,5},{8,10},{9,11},{10,... | collective-permute-start | bytes 1769480 | tf_op jit(solution)/shard_map/ppermute | solution.py:46
  42.1 26.6 %collective-permute-start.11 = (bf16[192,768]{1,0:T(8,128)(2,1)}, bf16[192,768]{1,0:T(8,128)(2,1)}, u32[]{:S(2)}, u32[]{:S(2)}) collective-permute-start(bf16[192,768]{1,0:T(8,128)(2,1)} %refs_0_.2), channel_id=1, source_target_pairs={{0,2},{1,3},{2,0},{3,1},{4,6},{5,7},{6,4},{7,5},{8,10},{9,11},{10,... | collective-permute-start | bytes 884744 | tf_op jit(solution)/shard_map/ppermute | solution.py:46
  63.8 7.9 %collective-permute-start.14 = (bf16[96,3072]{1,0:T(8,128)(2,1)}, bf16[96,3072]{1,0:T(8,128)(2,1)}, u32[]{:S(2)}, u32[]{:S(2)}) collective-permute-start(bf16[96,3072]{1,0:T(8,128)(2,1)} %collective-permute-done.13.refs_6_.refs_2_), channel_id=1, source_target_pairs={{0,1},{1,0},{2,3},{3,2},{4,5},{5,4},{6,7},{7,6},{8,9},{9,8},{10,11... | collective-permute-start | bytes 1769480 | tf_op jit(solution)/shard_map/ppermute | solution.py:46
  68.8 15.7 %collective-permute-start.17 = (bf16[384,768]{1,0:T(8,128)(2,1)S(1)}, bf16[384,768]{1,0:T(8,128)(2,1)S(1)}, u32[]{:S(2)}, u32[]{:S(2)}) collective-permute-start(bf16[384,768]{1,0:T(8,128)(2,1)S(1)} %constant_dynamic-slice_fusion.8), channel_id=1, source_target_pairs={{0,2},{1,3},{2,0},{3,1},{4,6},{5,7},{6,4},{7,5},{8,10},{9,11},{10,... | collective-permute-start | bytes 1769480 | tf_op jit(solution)/shard_map/ppermute | solution.py:46
  69.9 18.8 %collective-permute-start.15 = (bf16[96,3072]{1,0:T(8,128)(2,1)}, bf16[96,3072]{1,0:T(8,128)(2,1)S(1)}, u32[]{:S(2)}, u32[]{:S(2)}) collective-permute-start(bf16[96,3072]{1,0:T(8,128)(2,1)} %collective-permute-done.13.refs_6_.refs_2_), channel_id=1, source_target_pairs={{0,4},{4,0},{8,12},{12,8},{16,20},{20,16},{24,28},{28,24},{1,5},{5... | collective-permute-start | bytes 1769480 | tf_op jit(solution)/shard_map/ppermute | solution.py:46
  84.6 14.9 %collective-permute-start.19 = (bf16[384,768]{1,0:T(8,128)(2,1)S(1)}, bf16[384,768]{1,0:T(8,128)(2,1)S(1)}, u32[]{:S(2)}, u32[]{:S(2)}) collective-permute-start(bf16[384,768]{1,0:T(8,128)(2,1)S(1)} %collective-permute-done.17.refs_2_), channel_id=1, source_target_pairs={{0,4},{4,0},{8,12},{12,8},{16,20},{20,16},{24,28},{28,24},{1,5},{5... | collective-permute-start | bytes 1769480 | tf_op jit(solution)/shard_map/ppermute | solution.py:46
  99.4 5.3 %collective-permute-start.20 = (bf16[384,768]{1,0:T(8,128)(2,1)S(1)}, bf16[384,768]{1,0:T(8,128)(2,1)S(1)}, u32[]{:S(2)}, u32[]{:S(2)}) collective-permute-start(bf16[384,768]{1,0:T(8,128)(2,1)S(1)} %collective-permute-done.19.refs_4_), channel_id=1, source_target_pairs={{0,1},{1,0},{2,3},{3,2},{4,5},{5,4},{6,7},{7,6},{8,9},{9,8},{10,11... | collective-permute-start | bytes 1769480 | tf_op jit(solution)/shard_map/ppermute | solution.py:46
  99.5 5.3 %collective-permute-start.18 = (bf16[384,768]{1,0:T(8,128)(2,1)S(1)}, bf16[384,768]{1,0:T(8,128)(2,1)S(1)}, u32[]{:S(2)}, u32[]{:S(2)}) collective-permute-start(bf16[384,768]{1,0:T(8,128)(2,1)S(1)} %collective-permute-done.17.refs_2_), channel_id=1, source_target_pairs={{0,1},{1,0},{2,3},{3,2},{4,5},{5,4},{6,7},{7,6},{8,9},{9,8},{10,11... | collective-permute-start | bytes 1769480 | tf_op jit(solution)/shard_map/ppermute | solution.py:46
  104.8 14.2 %collective-permute-start.21 = (bf16[1536,768]{1,0:T(8,128)(2,1)}, bf16[1536,768]{1,0:T(8,128)(2,1)}, u32[]{:S(2)}, u32[]{:S(2)}) collective-permute-start(bf16[1536,768]{1,0:T(8,128)(2,1)} %convolution_convert_fusion.1), channel_id=1, source_target_pairs={{0,1},{1,0},{2,3},{3,2},{4,5},{5,4},{6,7},{7,6},{8,9},{9,8},{10,11... | collective-permute-start | bytes 7077896 | tf_op jit(solution)/shard_map/ppermute | solution.py:46
  116.5 7.5 %collective-permute-start.22 = (bf16[384,3072]{1,0:T(8,128)(2,1)}, bf16[384,3072]{1,0:T(8,128)(2,1)}, u32[]{:S(2)}, u32[]{:S(2)}) collective-permute-start(bf16[384,3072]{1,0:T(8,128)(2,1)} %convolution_convert_fusion), channel_id=1, source_target_pairs={{0,1},{1,0},{2,3},{3,2},{4,5},{5,4},{6,7},{7,6},{8,9},{9,8},{10,11... | collective-permute-start | bytes 7077896 | tf_op jit(solution)/shard_map/ppermute | solution.py:46
  123.4 30.7 %collective-permute-start.24 = (bf16[1,768,768]{2,1,0:T(8,128)(2,1)}, bf16[1,768,768]{2,1,0:T(8,128)(2,1)}, u32[]{:S(2)}, u32[]{:S(2)}) collective-permute-start(bf16[1,768,768]{2,1,0:T(8,128)(2,1)} %dynamic-slice_bitcast_fusion), channel_id=1, source_target_pairs={{0,2},{1,3},{2,0},{3,1},{4,6},{5,7},{6,4},{7,5},{8,10},{9,11},{10,... | collective-permute-start | bytes 3538952 | tf_op jit(solution)/shard_map/ppermute | solution.py:46
  136.9 29.2 %collective-permute-start.23 = (bf16[2,96,3072]{2,1,0:T(8,128)(2,1)}, bf16[2,96,3072]{2,1,0:T(8,128)(2,1)}, u32[]{:S(2)}, u32[]{:S(2)}) collective-permute-start(bf16[2,96,3072]{2,1,0:T(8,128)(2,1)} %constant_dynamic-slice_fusion.3), channel_id=1, source_target_pairs={{0,4},{4,0},{8,12},{12,8},{16,20},{20,16},{24,28},{28,24},{1,5},{5... | collective-permute-start | bytes 3538952 | tf_op jit(solution)/shard_map/ppermute | solution.py:46
  138.5 43.5 %collective-permute-start.28 = (bf16[512,768]{1,0:T(8,128)(2,1)S(1)}, bf16[512,768]{1,0:T(8,128)(2,1)}, u32[]{:S(2)}, u32[]{:S(2)}) collective-permute-start(bf16[512,768]{1,0:T(8,128)(2,1)S(1)} %convolution_convert_fusion.2.dout.refs_0_), channel_id=1, source_target_pairs={{2,0},{3,1},{6,4},{7,5},{10,8},{11,9},{14,12},{15,13},{18,16},{19,... | collective-permute-start | bytes 2359304 | tf_op jit(solution)/shard_map/ppermute | solution.py:59
  141.5 16.0 %collective-permute-start.25 = (bf16[384,768]{1,0:T(8,128)(2,1)}, bf16[384,768]{1,0:T(8,128)(2,1)}, u32[]{:S(2)}, u32[]{:S(2)}) collective-permute-start(bf16[384,768]{1,0:T(8,128)(2,1)} %convolution_convert_fusion.6), channel_id=1, source_target_pairs={{0,1},{1,0},{2,3},{3,2},{4,5},{5,4},{6,7},{7,6},{8,9},{9,8},{10,11... | collective-permute-start | bytes 1769480 | tf_op jit(solution)/shard_map/ppermute | solution.py:46
  151.1 30.8 %collective-permute-start.31 = (f32[6,8,512]{2,1,0:T(8,128)}, f32[6,8,512]{2,1,0:T(8,128)}, u32[]{:S(2)}, u32[]{:S(2)}) collective-permute-start(f32[6,8,512]{2,1,0:T(8,128)} %add.394.refs_4_), channel_id=1, source_target_pairs={{2,0},{3,1},{6,4},{7,5},{10,8},{11,9},{14,12},{15,13},{18,16},{19,... | collective-permute-start | bytes 294920 | tf_op jit(solution)/shard_map/ppermute | solution.py:59
  156.9 26.7 %collective-permute-start.26 = (bf16[384,768]{1,0:T(8,128)(2,1)}, bf16[384,768]{1,0:T(8,128)(2,1)}, u32[]{:S(2)}, u32[]{:S(2)}) collective-permute-start(bf16[384,768]{1,0:T(8,128)(2,1)} %dynamic-slice_bitcast_fusion.1), channel_id=1, source_target_pairs={{0,4},{4,0},{8,12},{12,8},{16,20},{20,16},{24,28},{28,24},{1,5},{5... | collective-permute-start | bytes 1769480 | tf_op jit(solution)/shard_map/ppermute | solution.py:46
  168.7 16.4 %collective-permute-start.27 = (bf16[1,96,3072]{2,1,0:T(8,128)(2,1)}, bf16[1,96,3072]{2,1,0:T(8,128)(2,1)}, u32[]{:S(2)}, u32[]{:S(2)}) collective-permute-start(bf16[1,96,3072]{2,1,0:T(8,128)(2,1)} %constant_dynamic-slice_fusion.2), channel_id=1, source_target_pairs={{0,2},{1,3},{2,0},{3,1},{4,6},{5,7},{6,4},{7,5},{8,10},{9,11},{10,... | collective-permute-start | bytes 1769480 | tf_op jit(solution)/shard_map/ppermute | solution.py:46
  178.4 9.9 %collective-permute-start.32 = (f32[6,8,512]{2,1,0:T(8,128)}, f32[6,8,512]{2,1,0:T(8,128)S(1)}, u32[]{:S(2)}, u32[]{:S(2)}) collective-permute-start(f32[6,8,512]{2,1,0:T(8,128)} %add.394.refs_4_), channel_id=1, source_target_pairs={{0,1},{1,0},{2,3},{3,2},{4,5},{5,4},{6,7},{7,6},{8,9},{9,8},{10,11... | collective-permute-start | bytes 294920 | tf_op jit(solution)/shard_map/ppermute | solution.py:46
  181.9 8.0 %collective-permute-start.33 = (f32[6,8,512]{2,1,0:T(8,128)}, f32[6,8,512]{2,1,0:T(8,128)S(1)}, u32[]{:S(2)}, u32[]{:S(2)}) collective-permute-start(f32[6,8,512]{2,1,0:T(8,128)} %collective-permute-done.31.refs_5_), channel_id=1, source_target_pairs={{0,1},{1,0},{2,3},{3,2},{4,5},{5,4},{6,7},{7,6},{8,9},{9,8},{10,11... | collective-permute-start | bytes 294920 | tf_op jit(solution)/shard_map/ppermute | solution.py:46
  182.0 25.8 %collective-permute-start.29 = (bf16[512,768]{1,0:T(8,128)(2,1)S(1)}, bf16[512,768]{1,0:T(8,128)(2,1)S(1)}, u32[]{:S(2)}, u32[]{:S(2)}) collective-permute-start(bf16[512,768]{1,0:T(8,128)(2,1)S(1)} %copy-done.30), channel_id=1, source_target_pairs={{0,1},{1,0},{2,3},{3,2},{4,5},{5,4},{6,7},{7,6},{8,9},{9,8},{10,11... | collective-permute-start | bytes 2359304 | tf_op jit(solution)/shard_map/ppermute | solution.py:46
  183.6 26.2 %collective-permute-start.30 = (bf16[512,768]{1,0:T(8,128)(2,1)}, bf16[512,768]{1,0:T(8,128)(2,1)}, u32[]{:S(2)}, u32[]{:S(2)}) collective-permute-start(bf16[512,768]{1,0:T(8,128)(2,1)} %collective-permute-done.28.refs_1_), channel_id=1, source_target_pairs={{0,1},{1,0},{2,3},{3,2},{4,5},{5,4},{6,7},{7,6},{8,9},{9,8},{10,11... | collective-permute-start | bytes 2359304 | tf_op jit(solution)/shard_map/ppermute | solution.py:46
  187.8 51.6 %collective-permute-start.35 = (bf16[384,768]{1,0:T(8,128)(2,1)}, bf16[384,768]{1,0:T(8,128)(2,1)}, u32[]{:S(2)}, u32[]{:S(2)}) collective-permute-start(bf16[384,768]{1,0:T(8,128)(2,1)} %convolution_convert_fusion.5), channel_id=1, source_target_pairs={{0,1},{1,0},{2,3},{3,2},{4,5},{5,4},{6,7},{7,6},{8,9},{9,8},{10,11... | collective-permute-start | bytes 1769480 | tf_op jit(solution)/shard_map/ppermute | solution.py:46
  188.2 35.8 %collective-permute-start.36 = (bf16[192,768]{1,0:T(8,128)(2,1)S(1)}, bf16[192,768]{1,0:T(8,128)(2,1)S(1)}, u32[]{:S(2)}, u32[]{:S(2)}) collective-permute-start(bf16[192,768]{1,0:T(8,128)(2,1)S(1)} %get-tuple-element.205), channel_id=1, source_target_pairs={{0,8},{4,12},{8,0},{12,4},{16,24},{20,28},{24,16},{28,20},{1,9},{5... | collective-permute-start | bytes 884744 | tf_op jit(solution)/shard_map/ppermute | solution.py:46
  189.9 34.1 %collective-permute-start.37 = (bf16[192,768]{1,0:T(8,128)(2,1)S(1)}, bf16[192,768]{1,0:T(8,128)(2,1)S(1)}, u32[]{:S(2)}, u32[]{:S(2)}) collective-permute-start(bf16[192,768]{1,0:T(8,128)(2,1)S(1)} %get-tuple-element.207), channel_id=1, source_target_pairs={{0,16},{4,20},{8,24},{12,28},{16,0},{20,4},{24,8},{28,12},{1,17},{... | collective-permute-start | bytes 884744 | tf_op jit(solution)/shard_map/ppermute | solution.py:46
  207.9 21.2 %collective-permute-start.38 = (bf16[192,768]{1,0:T(8,128)(2,1)S(1)}, bf16[192,768]{1,0:T(8,128)(2,1)S(1)}, u32[]{:S(2)}, u32[]{:S(2)}) collective-permute-start(bf16[192,768]{1,0:T(8,128)(2,1)S(1)} %get-tuple-element.206), channel_id=1, source_target_pairs={{0,24},{4,28},{8,16},{12,20},{16,8},{20,12},{24,0},{28,4},{1,25},{... | collective-permute-start | bytes 884744 | tf_op jit(solution)/shard_map/ppermute | solution.py:46
  223.9 17.6 %collective-permute-start.34 = (bf16[384,768]{1,0:T(8,128)(2,1)S(1)}, bf16[384,768]{1,0:T(8,128)(2,1)S(1)}, u32[]{:S(2)}, u32[]{:S(2)}) collective-permute-start(bf16[384,768]{1,0:T(8,128)(2,1)S(1)} %convolution_convert_fusion.4), channel_id=1, source_target_pairs={{0,1},{1,0},{2,3},{3,2},{4,5},{5,4},{6,7},{7,6},{8,9},{9,8},{10,11... | collective-permute-start | bytes 1769480 | tf_op jit(solution)/shard_map/ppermute | solution.py:46
  230.2 28.4 %collective-permute-start.59 = (bf16[192,768]{1,0:T(8,128)(2,1)S(1)}, bf16[192,768]{1,0:T(8,128)(2,1)S(1)}, u32[]{:S(2)}, u32[]{:S(2)}) collective-permute-start(bf16[192,768]{1,0:T(8,128)(2,1)S(1)} %fusion.45), channel_id=1, source_target_pairs={{0,8},{4,12},{8,0},{12,4},{16,24},{20,28},{24,16},{28,20},{1,9},{5... | collective-permute-start | bytes 884744 | tf_op jit(solution)/shard_map/ppermute | solution.py:46
  236.1 23.4 %collective-permute-start.61 = (bf16[192,768]{1,0:T(8,128)(2,1)S(1)}, bf16[192,768]{1,0:T(8,128)(2,1)S(1)}, u32[]{:S(2)}, u32[]{:S(2)}) collective-permute-start(bf16[192,768]{1,0:T(8,128)(2,1)S(1)} %fusion.45), channel_id=1, source_target_pairs={{0,16},{4,20},{8,24},{12,28},{16,0},{20,4},{24,8},{28,12},{1,17},{... | collective-permute-start | bytes 884744 | tf_op jit(solution)/shard_map/ppermute | solution.py:46
  238.1 22.2 %collective-permute-start.60 = (bf16[192,768]{1,0:T(8,128)(2,1)S(1)}, bf16[192,768]{1,0:T(8,128)(2,1)}, u32[]{:S(2)}, u32[]{:S(2)}) collective-permute-start(bf16[192,768]{1,0:T(8,128)(2,1)S(1)} %fusion.45), channel_id=1, source_target_pairs={{0,24},{4,28},{8,16},{12,20},{16,8},{20,12},{24,0},{28,4},{1,25},{... | collective-permute-start | bytes 884744 | tf_op jit(solution)/shard_map/ppermute | solution.py:46
  241.2 22.3 %collective-permute-start.42 = (bf16[1,384,768]{2,1,0:T(8,128)(2,1)S(1)}, bf16[1,384,768]{2,1,0:T(8,128)(2,1)}, u32[]{:S(2)}, u32[]{:S(2)}) collective-permute-start(bf16[1,384,768]{2,1,0:T(8,128)(2,1)S(1)} %get-tuple-element.204), channel_id=1, source_target_pairs={{0,2},{1,3},{2,0},{3,1},{4,6},{5,7},{6,4},{7,5},{8,10},{9,11},{10,... | collective-permute-start | bytes 1769480 | tf_op jit(solution)/shard_map/ppermute | solution.py:46
  243.5 19.9 %collective-permute-start.40 = (bf16[1,192,768]{2,1,0:T(8,128)(2,1)}, bf16[1,192,768]{2,1,0:T(8,128)(2,1)}, u32[]{:S(2)}, u32[]{:S(2)}) collective-permute-start(bf16[1,192,768]{2,1,0:T(8,128)(2,1)} %get-tuple-element.229), channel_id=1, source_target_pairs={{0,2},{1,3},{2,0},{3,1},{4,6},{5,7},{6,4},{7,5},{8,10},{9,11},{10,... | collective-permute-start | bytes 884744 | tf_op jit(solution)/shard_map/ppermute | solution.py:46
  258.6 13.6 %collective-permute-start.39 = (bf16[384,768]{1,0:T(8,128)(2,1)S(1)}, bf16[384,768]{1,0:T(8,128)(2,1)S(1)}, u32[]{:S(2)}, u32[]{:S(2)}) collective-permute-start(bf16[384,768]{1,0:T(8,128)(2,1)S(1)} %convolution_convert_fusion.3), channel_id=1, source_target_pairs={{0,1},{1,0},{2,3},{3,2},{4,5},{5,4},{6,7},{7,6},{8,9},{9,8},{10,11... | collective-permute-start | bytes 1769480 | tf_op jit(solution)/shard_map/ppermute | solution.py:46
  265.5 28.3 %collective-permute-start.43 = (bf16[192,768]{1,0:T(8,128)(2,1)}, bf16[192,768]{1,0:T(8,128)(2,1)}, u32[]{:S(2)}, u32[]{:S(2)}) collective-permute-start(bf16[192,768]{1,0:T(8,128)(2,1)} %dynamic-slice_bitcast_fusion.2), channel_id=1, source_target_pairs={{0,4},{4,0},{8,12},{12,8},{16,20},{20,16},{24,28},{28,24},{1,5},{5... | collective-permute-start | bytes 884744 | tf_op jit(solution)/shard_map/ppermute | solution.py:46
  273.6 8.8 %collective-permute-start.41 = (bf16[1,192,768]{2,1,0:T(8,128)(2,1)}, bf16[1,192,768]{2,1,0:T(8,128)(2,1)}, u32[]{:S(2)}, u32[]{:S(2)}) collective-permute-start(bf16[1,192,768]{2,1,0:T(8,128)(2,1)} %dynamic-slice_bitcast_fusion.3), channel_id=1, source_target_pairs={{0,2},{1,3},{2,0},{3,1},{4,6},{5,7},{6,4},{7,5},{8,10},{9,11},{10,... | collective-permute-start | bytes 884744 | tf_op jit(solution)/shard_map/ppermute | solution.py:46
  280.7 4.2 %collective-permute-start.63 = (f32[12,768]{1,0:T(8,128)S(1)}, f32[12,768]{1,0:T(8,128)S(1)}, u32[]{:S(2)}, u32[]{:S(2)}) collective-permute-start(f32[12,768]{1,0:T(8,128)S(1)} %concatenate.106), channel_id=1, source_target_pairs={{0,1},{1,0},{2,3},{3,2},{4,5},{5,4},{6,7},{7,6},{8,9},{9,8},{10,11... | collective-permute-start | bytes 110600 | tf_op jit(solution)/shard_map/ppermute | solution.py:46
  284.5 11.5 %collective-permute-start.44 = (bf16[192,768]{1,0:T(8,128)(2,1)S(1)}, bf16[192,768]{1,0:T(8,128)(2,1)S(1)}, u32[]{:S(2)}, u32[]{:S(2)}) collective-permute-start(bf16[192,768]{1,0:T(8,128)(2,1)S(1)} %bitcast.204), channel_id=1, source_target_pairs={{0,4},{4,0},{8,12},{12,8},{16,20},{20,16},{24,28},{28,24},{1,5},{5... | collective-permute-start | bytes 884744 | tf_op jit(solution)/shard_map/ppermute | solution.py:46
  284.9 9.9 %collective-permute-start.64 = (f32[12,768]{1,0:T(8,128)S(1)}, f32[12,768]{1,0:T(8,128)S(1)}, u32[]{:S(2)}, u32[]{:S(2)}) collective-permute-start(f32[12,768]{1,0:T(8,128)S(1)} %add.423), channel_id=1, source_target_pairs={{0,4},{4,0},{8,12},{12,8},{16,20},{20,16},{24,28},{28,24},{1,5},{5... | collective-permute-start | bytes 110600 | tf_op jit(solution)/shard_map/ppermute | solution.py:46
  293.5 49.0 %collective-permute-start.62 = (bf16[768,768]{1,0:T(8,128)(2,1)S(1)}, bf16[768,768]{1,0:T(8,128)(2,1)S(1)}, u32[]{:S(2)}, u32[]{:S(2)}) collective-permute-start(bf16[768,768]{1,0:T(8,128)(2,1)S(1)} %copy-done.57), channel_id=1, source_target_pairs={{0,4},{4,0},{8,12},{12,8},{16,20},{20,16},{24,28},{28,24},{1,5},{5... | collective-permute-start | bytes 3538952 | tf_op jit(solution)/shard_map/ppermute | solution.py:46
  294.8 28.1 %collective-permute-start.65 = (f32[12,768]{1,0:T(8,128)S(1)}, f32[12,768]{1,0:T(8,128)S(1)}, u32[]{:S(2)}, u32[]{:S(2)}) collective-permute-start(f32[12,768]{1,0:T(8,128)S(1)} %add.424), channel_id=1, source_target_pairs={{0,2},{1,3},{2,0},{3,1},{4,6},{5,7},{6,4},{7,5},{8,10},{9,11},{10,... | collective-permute-start | bytes 110600 | tf_op jit(solution)/shard_map/ppermute | solution.py:46
  296.3 11.4 %collective-permute-start.45 = (bf16[48,768]{1,0:T(8,128)(2,1)S(1)}, bf16[48,768]{1,0:T(8,128)(2,1)S(1)}, u32[]{:S(2)}, u32[]{:S(2)}) collective-permute-start(bf16[48,768]{1,0:T(8,128)(2,1)S(1)} %get-tuple-element.241), channel_id=1, source_target_pairs={{0,8},{4,12},{8,0},{12,4},{16,24},{20,28},{24,16},{28,20},{1,9},{5... | collective-permute-start | bytes 221192 | tf_op jit(solution)/shard_map/ppermute | solution.py:46
  300.7 9.0 %collective-permute-start.46 = (bf16[48,768]{1,0:T(8,128)(2,1)S(1)}, bf16[48,768]{1,0:T(8,128)(2,1)S(1)}, u32[]{:S(2)}, u32[]{:S(2)}) collective-permute-start(bf16[48,768]{1,0:T(8,128)(2,1)S(1)} %get-tuple-element.243), channel_id=1, source_target_pairs={{0,16},{4,20},{8,24},{12,28},{16,0},{20,4},{24,8},{28,12},{1,17},{... | collective-permute-start | bytes 221192 | tf_op jit(solution)/shard_map/ppermute | solution.py:46
  306.4 6.9 %collective-permute-start.47 = (bf16[48,768]{1,0:T(8,128)(2,1)S(1)}, bf16[48,768]{1,0:T(8,128)(2,1)S(1)}, u32[]{:S(2)}, u32[]{:S(2)}) collective-permute-start(bf16[48,768]{1,0:T(8,128)(2,1)S(1)} %get-tuple-element.242), channel_id=1, source_target_pairs={{0,24},{4,28},{8,16},{12,20},{16,8},{20,12},{24,0},{28,4},{1,25},{... | collective-permute-start | bytes 221192 | tf_op jit(solution)/shard_map/ppermute | solution.py:46
  307.8 8.2 %collective-permute-start.49 = (bf16[48,768]{1,0:T(8,128)(2,1)S(1)}, bf16[48,768]{1,0:T(8,128)(2,1)S(1)}, u32[]{:S(2)}, u32[]{:S(2)}) collective-permute-start(bf16[48,768]{1,0:T(8,128)(2,1)S(1)} %get-tuple-element.238), channel_id=1, source_target_pairs={{0,8},{4,12},{8,0},{12,4},{16,24},{20,28},{24,16},{28,20},{1,9},{5... | collective-permute-start | bytes 221192 | tf_op jit(solution)/shard_map/ppermute | solution.py:46
  309.7 7.2 %collective-permute-start.50 = (bf16[48,768]{1,0:T(8,128)(2,1)S(1)}, bf16[48,768]{1,0:T(8,128)(2,1)S(1)}, u32[]{:S(2)}, u32[]{:S(2)}) collective-permute-start(bf16[48,768]{1,0:T(8,128)(2,1)S(1)} %get-tuple-element.240), channel_id=1, source_target_pairs={{0,16},{4,20},{8,24},{12,28},{16,0},{20,4},{24,8},{28,12},{1,17},{... | collective-permute-start | bytes 221192 | tf_op jit(solution)/shard_map/ppermute | solution.py:46
  313.3 6.8 %collective-permute-start.51 = (bf16[48,768]{1,0:T(8,128)(2,1)S(1)}, bf16[48,768]{1,0:T(8,128)(2,1)S(1)}, u32[]{:S(2)}, u32[]{:S(2)}) collective-permute-start(bf16[48,768]{1,0:T(8,128)(2,1)S(1)} %get-tuple-element.239), channel_id=1, source_target_pairs={{0,24},{4,28},{8,16},{12,20},{16,8},{20,12},{24,0},{28,4},{1,25},{... | collective-permute-start | bytes 221192 | tf_op jit(solution)/shard_map/ppermute | solution.py:46
  316.0 9.8 %collective-permute-start.53 = (bf16[48,768]{1,0:T(8,128)(2,1)S(1)}, bf16[48,768]{1,0:T(8,128)(2,1)S(1)}, u32[]{:S(2)}, u32[]{:S(2)}) collective-permute-start(bf16[48,768]{1,0:T(8,128)(2,1)S(1)} %fusion.68), channel_id=1, source_target_pairs={{0,8},{4,12},{8,0},{12,4},{16,24},{20,28},{24,16},{28,20},{1,9},{5... | collective-permute-start | bytes 221192 | tf_op jit(solution)/shard_map/ppermute | solution.py:46
  316.9 8.9 %collective-permute-start.52 = (bf16[48,768]{1,0:T(8,128)(2,1)S(1)}, bf16[48,768]{1,0:T(8,128)(2,1)S(1)}, u32[]{:S(2)}, u32[]{:S(2)}) collective-permute-start(bf16[48,768]{1,0:T(8,128)(2,1)S(1)} %fusion.68), channel_id=1, source_target_pairs={{0,16},{4,20},{8,24},{12,28},{16,0},{20,4},{24,8},{28,12},{1,17},{... | collective-permute-start | bytes 221192 | tf_op jit(solution)/shard_map/ppermute | solution.py:46
  320.0 9.7 %collective-permute-start.48 = (bf16[48,768]{1,0:T(8,128)(2,1)S(1)}, bf16[48,768]{1,0:T(8,128)(2,1)S(1)}, u32[]{:S(2)}, u32[]{:S(2)}) collective-permute-start(bf16[48,768]{1,0:T(8,128)(2,1)S(1)} %fusion.68), channel_id=1, source_target_pairs={{0,24},{4,28},{8,16},{12,20},{16,8},{20,12},{24,0},{28,4},{1,25},{... | collective-permute-start | bytes 221192 | tf_op jit(solution)/shard_map/ppermute | solution.py:46
  322.9 9.2 %collective-permute-start.57 = (bf16[48,768]{1,0:T(8,128)(2,1)S(1)}, bf16[48,768]{1,0:T(8,128)(2,1)S(1)}, u32[]{:S(2)}, u32[]{:S(2)}) collective-permute-start(bf16[48,768]{1,0:T(8,128)(2,1)S(1)} %fusion.65), channel_id=1, source_target_pairs={{0,8},{4,12},{8,0},{12,4},{16,24},{20,28},{24,16},{28,20},{1,9},{5... | collective-permute-start | bytes 221192 | tf_op jit(solution)/shard_map/ppermute | solution.py:46
  325.8 6.7 %collective-permute-start.56 = (bf16[48,768]{1,0:T(8,128)(2,1)S(1)}, bf16[48,768]{1,0:T(8,128)(2,1)S(1)}, u32[]{:S(2)}, u32[]{:S(2)}) collective-permute-start(bf16[48,768]{1,0:T(8,128)(2,1)S(1)} %fusion.65), channel_id=1, source_target_pairs={{0,16},{4,20},{8,24},{12,28},{16,0},{20,4},{24,8},{28,12},{1,17},{... | collective-permute-start | bytes 221192 | tf_op jit(solution)/shard_map/ppermute | solution.py:46
  325.8 6.7 %collective-permute-start.55 = (bf16[48,768]{1,0:T(8,128)(2,1)S(1)}, bf16[48,768]{1,0:T(8,128)(2,1)S(1)}, u32[]{:S(2)}, u32[]{:S(2)}) collective-permute-start(bf16[48,768]{1,0:T(8,128)(2,1)S(1)} %fusion.65), channel_id=1, source_target_pairs={{0,24},{4,28},{8,16},{12,20},{16,8},{20,12},{24,0},{28,4},{1,25},{... | collective-permute-start | bytes 221192 | tf_op jit(solution)/shard_map/ppermute | solution.py:46
  329.8 9.1 %collective-permute-start.54 = (bf16[192,768]{1,0:T(8,128)(2,1)S(1)}, bf16[192,768]{1,0:T(8,128)(2,1)S(1)}, u32[]{:S(2)}, u32[]{:S(2)}) collective-permute-start(bf16[192,768]{1,0:T(8,128)(2,1)S(1)} %pad_maximum_fusion.12), channel_id=1, source_target_pairs={{0,4},{4,0},{8,12},{12,8},{16,20},{20,16},{24,28},{28,24},{1,5},{5... | collective-permute-start | bytes 884744 | tf_op jit(solution)/shard_map/ppermute | solution.py:46
  332.5 9.5 %collective-permute-start.58 = (bf16[192,768]{1,0:T(8,128)(2,1)S(1)}, bf16[192,768]{1,0:T(8,128)(2,1)S(1)}, u32[]{:S(2)}, u32[]{:S(2)}) collective-permute-start(bf16[192,768]{1,0:T(8,128)(2,1)S(1)} %pad_maximum_fusion.13), channel_id=1, source_target_pairs={{0,4},{4,0},{8,12},{12,8},{16,20},{20,16},{24,28},{28,24},{1,5},{5... | collective-permute-start | bytes 884744 | tf_op jit(solution)/shard_map/ppermute | solution.py:46
  342.5 4.2 %collective-permute-start.66 = (f32[12,768]{1,0:T(8,128)S(1)}, f32[12,768]{1,0:T(8,128)S(1)}, u32[]{:S(2)}, u32[]{:S(2)}) collective-permute-start(f32[12,768]{1,0:T(8,128)S(1)} %add_add_fusion.2), channel_id=1, source_target_pairs={{0,8},{4,12},{8,0},{12,4},{16,24},{20,28},{24,16},{28,20},{1,9},{5... | collective-permute-start | bytes 110600 | tf_op jit(solution)/shard_map/ppermute | solution.py:46
  346.7 5.6 %collective-permute-start.67 = (f32[12,768]{1,0:T(8,128)S(1)}, f32[12,768]{1,0:T(8,128)S(1)}, u32[]{:S(2)}, u32[]{:S(2)}) collective-permute-start(f32[12,768]{1,0:T(8,128)S(1)} %add.429), channel_id=1, source_target_pairs={{0,16},{4,20},{8,24},{12,28},{16,0},{20,4},{24,8},{28,12},{1,17},{... | collective-permute-start | bytes 110600 | tf_op jit(solution)/shard_map/ppermute | solution.py:46
  (98 other events, 657.0 us)
where the time goes:
time: 358 us; the launch traced here: 354 us
  starting transfers between devices  111 us (31%)
  Pallas kernels  62.8 us (18%)
  matrix products  59.9 us (17%)
  waiting for transfers between devices  52 us (15%)
  other arithmetic  35.9 us (10%)
  local copies, waits for them, and re-layouts  26.7 us (7%)
  between operations  5.96 us (2%)
    ppermute x65, starting transfers between devices, swap(): got = lax.ppermute(value, axis, [(i, i ^ mask) for i in range(size)])  107 us
    ppermute x65, waiting for transfers between devices, swap(): got = lax.ppermute(value, axis, [(i, i ^ mask) for i in range(size)])  52 us
    pallas_call x2, Pallas kernels, key_grads(): call(functools.partial(key_grad_kernel, size, tile), key_value_strips(cou...  24.6 us
    dot_general x12, matrix products, token_product(): return jnp.einsum('tc,te->ce', left, right, preferred_element_type=F32)  24.6 us
    dot_general x4, matrix products, add_rows(): return jnp.dot(left, piece, preferred_element_type=F32)  21.3 us
    pallas_call x2, Pallas kernels, query_grads(): call(functools.partial(query_grad_kernel, size, tile), [strip(count, firs...  15.6 us
    pallas_call x2, Pallas kernels, attend(): call(functools.partial(attend_kernel, size, tile, len(earlier) + len(read...  15 us
    dot_general x4, matrix products, back_rows(): return jnp.einsum('te,ce->tc', right, piece, preferred_element_type=F32)  13 us
  transfers between devices with their start and end apart: 68, of which 19 were waited for; matrix products, arithmetic and copies ran while one was open for 32% of the time, Pallas kernels for 18%

commit v1 on v0

--- a/solution.py
+++ b/solution.py
@@ -638,21 +638,21 @@
     mixed_one = key_grads(0, part, *heads, [after(dout_all[0], query_theirs, both_part)] + dout_all[1:], stats, *shapes)
 
     query_part = core_grad(query_theirs, normed_mine, after(both_queries, mixed_one), size)
-    pair_part = jnp.concatenate([query_part, out_part], axis=1)
-    pair_send, pair_keep = group_step(pair_part, bits_of(size) - 1, me)
     one_theirs = other_grad(normed_theirs, mixed_one)
     both_part = scatter_far(both_part, rep, reps, mixed_one)
     one_part = core_grad(one_theirs, normed_mine, mixed_one, size)
-    one_send, one_keep = group_step(one_part, bits_of(size) - 1, me)
+    pair_part = jnp.concatenate([query_part, out_part, one_part], axis=1)
+    pair_send, pair_keep = group_step(pair_part, bits_of(size) - 1, me)
     mixed_two = key_grads(
-        part, part, *heads, [after(dout_all[0], one_send, pair_send, both_part)] + dout_all[1:], stats, *shapes
+        part, part, *heads, [after(dout_all[0], pair_send, both_part)] + dout_all[1:], stats, *shapes
     )
 
     two_theirs = other_grad(normed_theirs, mixed_two)
     two_part = core_grad(two_theirs, normed_mine, mixed_two, size)
     two_send, two_keep = group_step(two_part, bits_of(size) - 1, me)
-    one_part = add_low(after(one_keep, two_send), swap(one_send, "grp", size, size // 2, mixed_two))
     pair_part = add_low(after(pair_keep, two_theirs), swap(pair_send, "grp", size, size // 2, mixed_two))
+    pair_rows = 2 * w_qkv.shape[0]
+    pair_part, one_part = pair_part[:, :pair_rows], pair_part[:, pair_rows:]
     pair_send, pair_keep = rep_halves(group_sum(pair_part, me, size)[0], rep)
     both_every = share_far(both_part, rep, reps, mixed_two)
 

time: 358 us -> 354 us (0.989)
  starting transfers between devices: 111 us -> 101 us
  waiting for transfers between devices: 52 us -> 60.5 us
    ppermute x65 -> x64, starting transfers between devices: 107 us -> 95.9 us  [swap(): got = lax.ppermute(value, axis, [(i, i ^ mask) for i in range(size)])]
    ppermute x65 -> x64, waiting for transfers between devices: 52 us -> 60.5 us  [swap(): got = lax.ppermute(value, axis, [(i, i ^ mask) for i in range(size)])]
    convert_element_type x7 -> x6, other arithmetic: 8.64 us -> 6.76 us  [add_low(): return (keep.astype(F32) + got.astype(F32)).astype(BF16)]
    unnamed x201 -> x193, local copies, waits for them, and re-layouts: 7.9 us -> 9.2 us
  transfers between devices with their start and end apart: 68 -> 67, of which waited for: 19 -> 20; matrix products, arithmetic and copies ran while one was open for 32% -> 31% of each run, Pallas kernels for 18% -> 18%
where the time goes in v1:
time: 354 us; the launch traced here: 351 us
  starting transfers between devices  101 us (29%)
  Pallas kernels  62.7 us (18%)
  waiting for transfers between devices  60.5 us (17%)
  matrix products  60.4 us (17%)
  other arithmetic  34.2 us (10%)
  local copies, waits for them, and re-layouts  26 us (7%)
  between operations  6.22 us (2%)
    ppermute x64, starting transfers between devices, swap(): got = lax.ppermute(value, axis, [(i, i ^ mask) for i in range(size)])  95.9 us
    ppermute x64, waiting for transfers between devices, swap(): got = lax.ppermute(value, axis, [(i, i ^ mask) for i in range(size)])  60.5 us
    pallas_call x2, Pallas kernels, key_grads(): call(functools.partial(key_grad_kernel, size, tile), key_value_strips(cou...  24.6 us
    dot_general x12, matrix products, token_product(): return jnp.einsum('tc,te->ce', left, right, preferred_element_type=F32)  24.4 us
    dot_general x4, matrix products, add_rows(): return jnp.dot(left, piece, preferred_element_type=F32)  21.4 us
    pallas_call x2, Pallas kernels, query_grads(): call(functools.partial(query_grad_kernel, size, tile), [strip(count, firs...  15.4 us
    pallas_call x2, Pallas kernels, attend(): call(functools.partial(attend_kernel, size, tile, len(earlier) + len(read...  15 us
    dot_general x4, matrix products, back_rows(): return jnp.einsum('te,ce->tc', right, piece, preferred_element_type=F32)  13.5 us
  transfers between devices with their start and end apart: 67, of which 20 were waited for; matrix products, arithmetic and copies ran while one was open for 31% of the time, Pallas kernels for 18%

profile of v1, /device:TPU:0, one launch (start us, length us, event | category | flops | bytes accessed | tf_op | source)
XLA Modules:
  0.0 350.6 jit_solution(2203788457379808167)
XLA Ops:
  1.8 3.0 collective-permute-start
  7.9 7.1 %collective-permute-done.refs_2_ = bf16[96,2304]{1,0:T(8,128)(2,1)S(1)} collective-permute-done((bf16[96,2304]{1,0:T(8,128)(2,1)S(1)}, bf16[96,2304]{1,0:T(8,128)(2,1)S(1)}, u32[]{:S(2)}, u32[]{:S(2)}) %collective-permute-start) | collective-permute-done | bytes 442400 | tf_op jit(solution)/shard_map/ppermute | solution.py:46
  15.0 1.7 collective-permute-start.1
  17.4 1.9 fusion.87
  27.3 8.1 %collective-permute-done.2.refs_4_ = bf16[96,2304]{1,0:T(8,128)(2,1)S(1)} collective-permute-done((bf16[96,2304]{1,0:T(8,128)(2,1)S(1)}, bf16[96,2304]{1,0:T(8,128)(2,1)S(1)}, u32[]{:S(2)}, u32[]{:S(2)}) %collective-permute-start.2) | collective-permute-done | bytes 442400 | tf_op jit(solution)/shard_map/ppermute | solution.py:46
  36.2 2.1 collective-permute-done.6.refs_3_
  39.1 2.2 shard_map.186
  41.7 1.7 collective-permute-start.11
  45.0 9.7 %add_convert_fusion.q_ref.k_ref.v_ref = bf16[2048,2304]{1,0:T(8,128)(2,1)} fusion(bf16[2048,768]{1,0:T(8,128)(2,1)S(1)} %pad_maximum_fusion, bf16[768,2304]{1,0:T(8,128)(2,1)S(1)} %shard_map.186, f32[2304]{0:T(1024)S(1)} %pad_maximum_fusion.23), kind=kOutput, calls=%fused_computation | convolution fusion | flops 7257194496 | bytes 16131072 | tf_op jit(solution)/shard_map/dot_general | solution.py:30
  54.9 7.6 %shard_map.187 = (f32[512,768]{1,0:T(8,128)S(1)}, bf16[512,768]{1,0:T(8,128)(2,1)S(1)}, f32[512,768]{1,0:T(8,128)S(1)}, f32[6,8,512]{2,1,0:T(8,128)S(1)}) custom-call(s32[3]{0:T(128)S(1)} %pad_add_fusion.info, bf16[2048,2304]{1,0:T(8,128)(2,1)} %add_convert_fusion.q_ref.k_ref.v_ref, bf16[2048,2304]{1,0:T(8,128)(2,1)} %add_convert_fusion.q_ref.k_ref.v_ref, ...), custom_call_target="tpu_custom_call" | custom-call | flops 3221225472 | bytes 8388608 | tf_op jit(solution)/shard_map/pallas_call | solution.py:466
  63.4 3.7 %collective-permute-start.14 = (bf16[96,3072]{1,0:T(8,128)(2,1)}, bf16[96,3072]{1,0:T(8,128)(2,1)}, u32[]{:S(2)}, u32[]{:S(2)}) collective-permute-start(bf16[96,3072]{1,0:T(8,128)(2,1)} %collective-permute-done.13.refs_6_.refs_2_), channel_id=1, source_target_pairs={{0,1},{1,0},{2,3},{3,2},{4,5},{5,4},{6,7},{7,6},{8,9},{9,8},{10,11... | collective-permute-start | bytes 1769480 | tf_op jit(solution)/shard_map/ppermute | solution.py:46
  69.6 1.8 collective-permute-start.15
  71.4 7.3 %shard_map.188 = (f32[512,768]{1,0:T(8,128)S(1)}, bf16[512,768]{1,0:T(8,128)(2,1)S(1)}, f32[512,768]{1,0:T(8,128)S(1)}, f32[6,8,512]{2,1,0:T(8,128)S(1)}) custom-call(s32[3]{0:T(128)S(1)} %pad_add_fusion.info, bf16[2048,2304]{1,0:T(8,128)(2,1)} %add_convert_fusion.q_ref.k_ref.v_ref, ...), custom_call_target="tpu_custom_call", output_to_operand_aliasing={{0}: (6, {}), {1}: (7, {}), {2}: (8, {}), {3}: (9, {})} | custom-call | flops 3221225472 | bytes 8388608 | tf_op jit(solution)/shard_map/pallas_call | solution.py:466
  78.8 5.4 %collective-permute-done.17.refs_2_ = bf16[384,768]{1,0:T(8,128)(2,1)S(1)} collective-permute-done((bf16[384,768]{1,0:T(8,128)(2,1)S(1)}, bf16[384,768]{1,0:T(8,128)(2,1)S(1)}, u32[]{:S(2)}, u32[]{:S(2)}) %collective-permute-start.17) | collective-permute-done | bytes 589856 | tf_op jit(solution)/shard_map/ppermute | solution.py:46
  85.7 1.6 shard_map.189
  90.6 2.3 shard_map.190
  93.0 4.0 %multiply_convert_fusion = (bf16[512,3072]{1,0:T(8,128)(2,1)S(1)}, f32[512,3072]{1,0:T(8,128)S(1)}) fusion(f32[3072]{0:T(1024)S(1)} %copy-done.86, bf16[512,768]{1,0:T(8,128)(2,1)S(1)} %add_convert_fusion.6, bf16[768,3072]{1,0:T(8,128)(2,1)S(1)} %shard_map.190), kind=kOutput, calls=%fused_computation.11 | convolution fusion | flops 2431647744 | bytes 14954496 | tf_op jit(solution)/shard_map/dot_general | solution.py:30
  97.0 2.1 collective-permute-done.19.refs_4_
  101.6 2.8 convolution_convert_fusion.1
  104.5 1.6 shard_map.191
  106.1 7.1 %convert_reduce_fusion = (f32[3072]{0:T(1024)}, bf16[512,3072]{1,0:T(8,128)(2,1)S(1)}) fusion(f32[512,3072]{1,0:T(8,128)S(1)} %get-tuple-element.251, f32[3072]{0:T(1024)S(1)} %copy-done.86, bf16[512,768]{1,0:T(8,128)(2,1)S(1)} %bitcast.188, bf16[3072,768]{1,0:T(8,128)(2,1)S(1)} %shard_map.191), kind=kOutput, calls=%fused_computation.10 | convolution fusion | flops 2452091904 | bytes 14966784 | tf_op jit(solution)/shard_map/te,ce->tc/dot_general | solution.py:34
  113.2 3.0 convolution_convert_fusion
  118.0 3.2 add_convert_fusion.2
  123.1 4.1 %add_convert_fusion.1 = bf16[384,3072]{1,0:T(8,128)(2,1)S(1)} fusion(bf16[384,3072]{1,0:T(8,128)(2,1)} %collective-permute-done.22, bf16[512,3072]{1,0:T(8,128)(2,1)S(1)} %copy-done.37, pred[]{:T(512)S(6)} %eq.14, bf16[512,192]{1,0:T(8,128)(2,1)S(1)} %copy-done.54, bf16[512,192]{1,0:T(8,128)(2,1)S(1)} %copy-done.56, bf16[512,192]{1,0:T(8,128)(2,1)S(1)} %copy-done.58, ...), kind=kOutput, calls=%fused_computation.13 | convolution fusion | flops 1213267968 | bytes 8650753 | tf_op jit(solution)/shard_map/tc,te->ce/dot_general | solution.py:38
  129.7 3.5 multiply_reduce_fusion
  142.2 7.6 %shard_map.192 = bf16[512,384]{1,0:T(8,128)(2,1)} custom-call(s32[3]{0:T(128)} %copy-done.25, bf16[2048,2304]{1,0:T(8,128)(2,1)} %add_convert_fusion.q_ref.k_ref.v_ref, bf16[2048,2304]{1,0:T(8,128)(2,1)} %add_convert_fusion.q_ref.k_ref.v_ref, bf16[2048,2304]{1,0:T(8,128)(2,1)} %add_convert_fusion.q_ref.k_ref.v_ref, bf16[512,768]{1,0:T(8,128)(2,1)} %copy-done.29, ...), custom_call_target="tpu_custom_call" | custom-call | flops 4831838208 | bytes 8388608 | tf_op jit(solution)/shard_map/pallas_call | solution.py:484
  150.5 1.6 collective-permute-start.31
  152.1 1.9 fusion.7
  155.9 2.6 add_convert_fusion.8
  158.5 7.3 %collective-permute-done.23 = bf16[2,96,3072]{2,1,0:T(8,128)(2,1)} collective-permute-done((bf16[2,96,3072]{2,1,0:T(8,128)(2,1)}, bf16[2,96,3072]{2,1,0:T(8,128)(2,1)}, u32[]{:S(2)}, u32[]{:S(2)}) %collective-permute-start.23) | collective-permute-done | bytes 1179680 | tf_op jit(solution)/shard_map/ppermute | solution.py:46
  165.7 1.7 add_convert_fusion.3
  168.5 7.8 %shard_map.193 = bf16[512,384]{1,0:T(8,128)(2,1)} custom-call(s32[3]{0:T(128)} %copy-done.25, bf16[2048,2304]{1,0:T(8,128)(2,1)} %add_convert_fusion.q_ref.k_ref.v_ref, bf16[2048,2304]{1,0:T(8,128)(2,1)} %add_convert_fusion.q_ref.k_ref.v_ref, bf16[2048,2304]{1,0:T(8,128)(2,1)} %add_convert_fusion.q_ref.k_ref.v_ref, bf16[512,768]{1,0:T(8,128)(2,1)} %copy-done.29, ...), custom_call_target="tpu_custom_call" | custom-call | flops 4831838208 | bytes 8388608 | tf_op jit(solution)/shard_map/pallas_call | solution.py:484
  176.3 3.5 %collective-permute-start.32 = (f32[6,8,512]{2,1,0:T(8,128)}, f32[6,8,512]{2,1,0:T(8,128)S(1)}, u32[]{:S(2)}, u32[]{:S(2)}) collective-permute-start(f32[6,8,512]{2,1,0:T(8,128)} %add.389.refs_4_), channel_id=1, source_target_pairs={{0,1},{1,0},{2,3},{3,2},{4,5},{5,4},{6,7},{7,6},{8,9},{9,8},{10,11... | collective-permute-start | bytes 294920 | tf_op jit(solution)/shard_map/ppermute | solution.py:46
  186.8 17.5 %collective-permute-start.36 = (bf16[192,768]{1,0:T(8,128)(2,1)}, bf16[192,768]{1,0:T(8,128)(2,1)}, u32[]{:S(2)}, u32[]{:S(2)}) collective-permute-start(bf16[192,768]{1,0:T(8,128)(2,1)} %get-tuple-element.201), channel_id=1, source_target_pairs={{0,8},{4,12},{8,0},{12,4},{16,24},{20,28},{24,16},{28,20},{1,9},{5... | collective-permute-start | bytes 884744 | tf_op jit(solution)/shard_map/ppermute | solution.py:46
  205.0 1.9 collective-permute-start.38
  206.9 12.3 %shard_map.194 = bf16[512,768]{1,0:T(8,128)(2,1)} custom-call(s32[3]{0:T(128)} %copy-done.25, bf16[2048,2304]{1,0:T(8,128)(2,1)} %add_convert_fusion.q_ref.k_ref.v_ref, bf16[2048,2304]{1,0:T(8,128)(2,1)} %add_convert_fusion.q_ref.k_ref.v_ref, bf16[2048,2304]{1,0:T(8,128)(2,1)} %add_convert_fusion.q_ref.k_ref.v_ref, s32[512,128]{1,0:T(8,128)} %copy-done.2, ...), custom_call_target="tpu_custom_call" | custom-call | flops 6442450944 | bytes 8388608 | tf_op jit(solution)/shard_map/pallas_call | solution.py:499
  219.2 1.7 convolution_convert_fusion.4
  221.1 5.6 %collective-permute-done.37 = bf16[192,768]{1,0:T(8,128)(2,1)} collective-permute-done((bf16[192,768]{1,0:T(8,128)(2,1)S(1)}, bf16[192,768]{1,0:T(8,128)(2,1)}, u32[]{:S(2)}, u32[]{:S(2)}) %collective-permute-start.37) | collective-permute-done | bytes 294944 | tf_op jit(solution)/shard_map/ppermute | solution.py:46
  228.0 6.7 %collective-permute-start.58 = (bf16[192,768]{1,0:T(8,128)(2,1)S(1)}, bf16[192,768]{1,0:T(8,128)(2,1)S(1)}, u32[]{:S(2)}, u32[]{:S(2)}) collective-permute-start(bf16[192,768]{1,0:T(8,128)(2,1)S(1)} %fusion.43), channel_id=1, source_target_pairs={{0,8},{4,12},{8,0},{12,4},{16,24},{20,28},{24,16},{28,20},{1,9},{5... | collective-permute-start | bytes 884744 | tf_op jit(solution)/shard_map/ppermute | solution.py:46
  234.8 2.4 collective-permute-start.59
  237.2 1.6 fusion.28
  241.0 7.5 %collective-permute-start.39 = (bf16[1,576,768]{2,1,0:T(8,128)(2,1)}, bf16[1,576,768]{2,1,0:T(8,128)(2,1)}, u32[]{:S(2)}, u32[]{:S(2)}) collective-permute-start(bf16[1,576,768]{2,1,0:T(8,128)(2,1)} %get-tuple-element.182), channel_id=1, source_target_pairs={{0,2},{1,3},{2,0},{3,1},{4,6},{5,7},{6,4},{7,5},{8,10},{9,11},{10,... | collective-permute-start | bytes 2654216 | tf_op jit(solution)/shard_map/ppermute | solution.py:46
  248.6 12.3 %shard_map.195 = bf16[512,768]{1,0:T(8,128)(2,1)} custom-call(s32[3]{0:T(128)} %copy-done.25, bf16[2048,2304]{1,0:T(8,128)(2,1)} %add_convert_fusion.q_ref.k_ref.v_ref, bf16[2048,2304]{1,0:T(8,128)(2,1)} %add_convert_fusion.q_ref.k_ref.v_ref, bf16[2048,2304]{1,0:T(8,128)(2,1)} %add_convert_fusion.q_ref.k_ref.v_ref, s32[512,128]{1,0:T(8,128)} %copy-done.2, ...), custom_call_target="tpu_custom_call" | custom-call | flops 6442450944 | bytes 8388608 | tf_op jit(solution)/shard_map/pallas_call | solution.py:499
  260.9 1.6 convolution_convert_fusion.3
  267.8 3.1 collective-permute-start.41
  274.2 2.1 fusion.20
  277.9 1.9 add_bitcast_fusion
  284.4 6.8 %add_convert_fusion.5 = bf16[512,768]{1,0:T(8,128)(2,1)} fusion(f32[512,768]{1,0:T(8,128)S(1)} %copy-done.33, bf16[512,3072]{1,0:T(8,128)(2,1)} %copy-done.42, bf16[3072,768]{1,0:T(8,128)(2,1)} %copy-done.7, f32[768]{0:T(1024)S(1)} %fusion.97), kind=kOutput, calls=%fused_computation.49 | convolution fusion | flops 2417098752 | bytes 10226688 | tf_op jit(solution)/shard_map/dot_general | solution.py:30
  293.2 8.4 %collective-permute-start.44 = (bf16[48,768]{1,0:T(8,128)(2,1)S(1)}, bf16[48,768]{1,0:T(8,128)(2,1)S(1)}, u32[]{:S(2)}, u32[]{:S(2)}) collective-permute-start(bf16[48,768]{1,0:T(8,128)(2,1)S(1)} %get-tuple-element.235), channel_id=1, source_target_pairs={{0,8},{4,12},{8,0},{12,4},{16,24},{20,28},{24,16},{28,20},{1,9},{5... | collective-permute-start | bytes 221192 | tf_op jit(solution)/shard_map/ppermute | solution.py:46
  301.6 2.4 collective-permute-start.46
  304.1 2.4 collective-permute-start.48
  306.4 3.4 collective-permute-done.45
  311.0 2.4 collective-permute-start.52
  313.4 3.4 collective-permute-done.49
  318.1 2.6 collective-permute-start.56
  322.2 1.6 collective-permute-done.51
  325.3 2.4 collective-permute-done.55
  327.7 2.2 collective-permute-done.54
  331.1 2.9 collective-permute-done.53
  335.1 2.1 collective-permute-done.57
  337.6 3.0 collective-permute-start.65
  340.7 1.7 maximum_convert_fusion
  344.2 1.6 maximum_convert_fusion.1
  345.8 2.5 collective-permute-done.66
  (411 shorter events, 81.3 us)
Async XLA Ops:
  1.8 13.2 %collective-permute-start = (bf16[96,2304]{1,0:T(8,128)(2,1)S(1)}, bf16[96,2304]{1,0:T(8,128)(2,1)S(1)}, u32[]{:S(2)}, u32[]{:S(2)}) collective-permute-start(bf16[96,2304]{1,0:T(8,128)(2,1)S(1)} %constant_dynamic-slice_fusion.12), channel_id=1, source_target_pairs={{0,2},{1,3},{2,0},{3,1},{4,6},{5,7},{6,4},{7,5},{8,10},{9,11},{10,... | collective-permute-start | bytes 1327112 | tf_op jit(solution)/shard_map/ppermute | solution.py:46
  15.0 20.4 %collective-permute-start.1 = (bf16[512,768]{1,0:T(8,128)(2,1)}, bf16[512,768]{1,0:T(8,128)(2,1)}, u32[]{:S(2)}, u32[]{:S(2)}) collective-permute-start(bf16[512,768]{1,0:T(8,128)(2,1)} %fusion.17), channel_id=1, source_target_pairs={{0,2},{1,3},{2,0},{3,1},{4,6},{5,7},{6,4},{7,5},{8,10},{9,11},{10,... | collective-permute-start | bytes 2359304 | tf_op jit(solution)/shard_map/ppermute | solution.py:59
  16.8 21.7 %collective-permute-start.5 = (bf16[192,2304]{1,0:T(8,128)(2,1)S(1)}, bf16[192,2304]{1,0:T(8,128)(2,1)S(1)}, u32[]{:S(2)}, u32[]{:S(2)}) collective-permute-start(bf16[192,2304]{1,0:T(8,128)(2,1)S(1)} %copy-done.19), channel_id=1, source_target_pairs={{0,1},{1,0},{2,3},{3,2},{4,5},{5,4},{6,7},{7,6},{8,9},{9,8},{10,11... | collective-permute-start | bytes 2654216 | tf_op jit(solution)/shard_map/ppermute | solution.py:46
  22.8 12.6 %collective-permute-start.2 = (bf16[96,2304]{1,0:T(8,128)(2,1)S(1)}, bf16[96,2304]{1,0:T(8,128)(2,1)S(1)}, u32[]{:S(2)}, u32[]{:S(2)}) collective-permute-start(bf16[96,2304]{1,0:T(8,128)(2,1)S(1)} %collective-permute-done.refs_2_), channel_id=1, source_target_pairs={{0,4},{4,0},{8,12},{12,8},{16,20},{20,16},{24,28},{28,24},{1,5},{5... | collective-permute-start | bytes 1327112 | tf_op jit(solution)/shard_map/ppermute | solution.py:46
  27.1 14.3 %collective-permute-start.3 = (bf16[512,768]{1,0:T(8,128)(2,1)}, bf16[512,768]{1,0:T(8,128)(2,1)S(1)}, u32[]{:S(2)}, u32[]{:S(2)}) collective-permute-start(bf16[512,768]{1,0:T(8,128)(2,1)} %fusion.17), channel_id=1, source_target_pairs={{0,1},{1,0},{2,3},{3,2},{4,5},{5,4},{6,7},{7,6},{8,9},{9,8},{10,11... | collective-permute-start | bytes 2359304 | tf_op jit(solution)/shard_map/ppermute | solution.py:46
  35.4 6.3 %collective-permute-start.4 = (bf16[512,768]{1,0:T(8,128)(2,1)}, bf16[512,768]{1,0:T(8,128)(2,1)S(1)}, u32[]{:S(2)}, u32[]{:S(2)}) collective-permute-start(bf16[512,768]{1,0:T(8,128)(2,1)} %collective-permute-done.1), channel_id=1, source_target_pairs={{0,1},{1,0},{2,3},{3,2},{4,5},{5,4},{6,7},{7,6},{8,9},{9,8},{10,11... | collective-permute-start | bytes 2359304 | tf_op jit(solution)/shard_map/ppermute | solution.py:46
  36.0 3.0 collective-permute-start.7
  38.3 16.4 %collective-permute-start.9 = (bf16[192,3072]{1,0:T(8,128)(2,1)S(1)}, bf16[192,3072]{1,0:T(8,128)(2,1)S(1)}, u32[]{:S(2)}, u32[]{:S(2)}) collective-permute-start(bf16[192,3072]{1,0:T(8,128)(2,1)S(1)} %copy-done.15), channel_id=1, source_target_pairs={{0,1},{1,0},{2,3},{3,2},{4,5},{5,4},{6,7},{7,6},{8,9},{9,8},{10,11... | collective-permute-start | bytes 3538952 | tf_op jit(solution)/shard_map/ppermute | solution.py:46
  38.5 16.3 %collective-permute-start.8 = (bf16[192,768]{1,0:T(8,128)(2,1)}, bf16[192,768]{1,0:T(8,128)(2,1)S(1)}, u32[]{:S(2)}, u32[]{:S(2)}) collective-permute-start(bf16[192,768]{1,0:T(8,128)(2,1)} %refs_0_.2), channel_id=1, source_target_pairs={{0,1},{1,0},{2,3},{3,2},{4,5},{5,4},{6,7},{7,6},{8,9},{9,8},{10,11... | collective-permute-start | bytes 884744 | tf_op jit(solution)/shard_map/ppermute | solution.py:46
  39.0 15.8 %collective-permute-start.10 = (bf16[768,768]{1,0:T(8,128)(2,1)S(1)}, bf16[768,768]{1,0:T(8,128)(2,1)S(1)}, u32[]{:S(2)}, u32[]{:S(2)}) collective-permute-start(bf16[768,768]{1,0:T(8,128)(2,1)S(1)} %copy-done.17), channel_id=1, source_target_pairs={{0,1},{1,0},{2,3},{3,2},{4,5},{5,4},{6,7},{7,6},{8,9},{9,8},{10,11... | collective-permute-start | bytes 3538952 | tf_op jit(solution)/shard_map/ppermute | solution.py:46
  41.3 22.1 %collective-permute-start.13 = (bf16[96,3072]{1,0:T(8,128)(2,1)S(1)}, bf16[96,3072]{1,0:T(8,128)(2,1)}, u32[]{:S(2)}, u32[]{:S(2)}) collective-permute-start(bf16[96,3072]{1,0:T(8,128)(2,1)S(1)} %constant_dynamic-slice_fusion.11), channel_id=1, source_target_pairs={{0,2},{1,3},{2,0},{3,1},{4,6},{5,7},{6,4},{7,5},{8,10},{9,11},{10,... | collective-permute-start | bytes 1769480 | tf_op jit(solution)/shard_map/ppermute | solution.py:46
  41.7 26.7 %collective-permute-start.11 = (bf16[192,768]{1,0:T(8,128)(2,1)}, bf16[192,768]{1,0:T(8,128)(2,1)}, u32[]{:S(2)}, u32[]{:S(2)}) collective-permute-start(bf16[192,768]{1,0:T(8,128)(2,1)} %refs_0_.2), channel_id=1, source_target_pairs={{0,2},{1,3},{2,0},{3,1},{4,6},{5,7},{6,4},{7,5},{8,10},{9,11},{10,... | collective-permute-start | bytes 884744 | tf_op jit(solution)/shard_map/ppermute | solution.py:46
  63.4 7.9 %collective-permute-start.14 = (bf16[96,3072]{1,0:T(8,128)(2,1)}, bf16[96,3072]{1,0:T(8,128)(2,1)}, u32[]{:S(2)}, u32[]{:S(2)}) collective-permute-start(bf16[96,3072]{1,0:T(8,128)(2,1)} %collective-permute-done.13.refs_6_.refs_2_), channel_id=1, source_target_pairs={{0,1},{1,0},{2,3},{3,2},{4,5},{5,4},{6,7},{7,6},{8,9},{9,8},{10,11... | collective-permute-start | bytes 1769480 | tf_op jit(solution)/shard_map/ppermute | solution.py:46
  68.5 15.7 %collective-permute-start.17 = (bf16[384,768]{1,0:T(8,128)(2,1)S(1)}, bf16[384,768]{1,0:T(8,128)(2,1)S(1)}, u32[]{:S(2)}, u32[]{:S(2)}) collective-permute-start(bf16[384,768]{1,0:T(8,128)(2,1)S(1)} %constant_dynamic-slice_fusion.10), channel_id=1, source_target_pairs={{0,2},{1,3},{2,0},{3,1},{4,6},{5,7},{6,4},{7,5},{8,10},{9,11},{10,... | collective-permute-start | bytes 1769480 | tf_op jit(solution)/shard_map/ppermute | solution.py:46
  69.6 18.9 %collective-permute-start.15 = (bf16[96,3072]{1,0:T(8,128)(2,1)}, bf16[96,3072]{1,0:T(8,128)(2,1)S(1)}, u32[]{:S(2)}, u32[]{:S(2)}) collective-permute-start(bf16[96,3072]{1,0:T(8,128)(2,1)} %collective-permute-done.13.refs_6_.refs_2_), channel_id=1, source_target_pairs={{0,4},{4,0},{8,12},{12,8},{16,20},{20,16},{24,28},{28,24},{1,5},{5... | collective-permute-start | bytes 1769480 | tf_op jit(solution)/shard_map/ppermute | solution.py:46
  84.2 14.9 %collective-permute-start.19 = (bf16[384,768]{1,0:T(8,128)(2,1)S(1)}, bf16[384,768]{1,0:T(8,128)(2,1)S(1)}, u32[]{:S(2)}, u32[]{:S(2)}) collective-permute-start(bf16[384,768]{1,0:T(8,128)(2,1)S(1)} %collective-permute-done.17.refs_2_), channel_id=1, source_target_pairs={{0,4},{4,0},{8,12},{12,8},{16,20},{20,16},{24,28},{28,24},{1,5},{5... | collective-permute-start | bytes 1769480 | tf_op jit(solution)/shard_map/ppermute | solution.py:46
  99.1 5.3 %collective-permute-start.20 = (bf16[384,768]{1,0:T(8,128)(2,1)S(1)}, bf16[384,768]{1,0:T(8,128)(2,1)S(1)}, u32[]{:S(2)}, u32[]{:S(2)}) collective-permute-start(bf16[384,768]{1,0:T(8,128)(2,1)S(1)} %collective-permute-done.19.refs_4_), channel_id=1, source_target_pairs={{0,1},{1,0},{2,3},{3,2},{4,5},{5,4},{6,7},{7,6},{8,9},{9,8},{10,11... | collective-permute-start | bytes 1769480 | tf_op jit(solution)/shard_map/ppermute | solution.py:46
  99.1 5.3 %collective-permute-start.18 = (bf16[384,768]{1,0:T(8,128)(2,1)S(1)}, bf16[384,768]{1,0:T(8,128)(2,1)S(1)}, u32[]{:S(2)}, u32[]{:S(2)}) collective-permute-start(bf16[384,768]{1,0:T(8,128)(2,1)S(1)} %collective-permute-done.17.refs_2_), channel_id=1, source_target_pairs={{0,1},{1,0},{2,3},{3,2},{4,5},{5,4},{6,7},{7,6},{8,9},{9,8},{10,11... | collective-permute-start | bytes 1769480 | tf_op jit(solution)/shard_map/ppermute | solution.py:46
  104.4 13.6 %collective-permute-start.21 = (bf16[1536,768]{1,0:T(8,128)(2,1)}, bf16[1536,768]{1,0:T(8,128)(2,1)}, u32[]{:S(2)}, u32[]{:S(2)}) collective-permute-start(bf16[1536,768]{1,0:T(8,128)(2,1)} %convolution_convert_fusion.1), channel_id=1, source_target_pairs={{0,1},{1,0},{2,3},{3,2},{4,5},{5,4},{6,7},{7,6},{8,9},{9,8},{10,11... | collective-permute-start | bytes 7077896 | tf_op jit(solution)/shard_map/ppermute | solution.py:46
  116.2 6.9 %collective-permute-start.22 = (bf16[384,3072]{1,0:T(8,128)(2,1)}, bf16[384,3072]{1,0:T(8,128)(2,1)}, u32[]{:S(2)}, u32[]{:S(2)}) collective-permute-start(bf16[384,3072]{1,0:T(8,128)(2,1)} %convolution_convert_fusion), channel_id=1, source_target_pairs={{0,1},{1,0},{2,3},{3,2},{4,5},{5,4},{6,7},{7,6},{8,9},{9,8},{10,11... | collective-permute-start | bytes 7077896 | tf_op jit(solution)/shard_map/ppermute | solution.py:46
  122.5 29.7 %collective-permute-start.24 = (bf16[1,768,768]{2,1,0:T(8,128)(2,1)}, bf16[1,768,768]{2,1,0:T(8,128)(2,1)}, u32[]{:S(2)}, u32[]{:S(2)}) collective-permute-start(bf16[1,768,768]{2,1,0:T(8,128)(2,1)} %dynamic-slice_bitcast_fusion), channel_id=1, source_target_pairs={{0,2},{1,3},{2,0},{3,1},{4,6},{5,7},{6,4},{7,5},{8,10},{9,11},{10,... | collective-permute-start | bytes 3538952 | tf_op jit(solution)/shard_map/ppermute | solution.py:46
  136.5 29.2 %collective-permute-start.23 = (bf16[2,96,3072]{2,1,0:T(8,128)(2,1)}, bf16[2,96,3072]{2,1,0:T(8,128)(2,1)}, u32[]{:S(2)}, u32[]{:S(2)}) collective-permute-start(bf16[2,96,3072]{2,1,0:T(8,128)(2,1)} %constant_dynamic-slice_fusion.5), channel_id=1, source_target_pairs={{0,4},{4,0},{8,12},{12,8},{16,20},{20,16},{24,28},{28,24},{1,5},{5... | collective-permute-start | bytes 3538952 | tf_op jit(solution)/shard_map/ppermute | solution.py:46
  138.1 41.8 %collective-permute-start.28 = (bf16[512,768]{1,0:T(8,128)(2,1)S(1)}, bf16[512,768]{1,0:T(8,128)(2,1)}, u32[]{:S(2)}, u32[]{:S(2)}) collective-permute-start(bf16[512,768]{1,0:T(8,128)(2,1)S(1)} %convolution_convert_fusion.2.dout.refs_0_), channel_id=1, source_target_pairs={{2,0},{3,1},{6,4},{7,5},{10,8},{11,9},{14,12},{15,13},{18,16},{19,... | collective-permute-start | bytes 2359304 | tf_op jit(solution)/shard_map/ppermute | solution.py:59
  141.1 14.8 %collective-permute-start.25 = (bf16[384,768]{1,0:T(8,128)(2,1)}, bf16[384,768]{1,0:T(8,128)(2,1)}, u32[]{:S(2)}, u32[]{:S(2)}) collective-permute-start(bf16[384,768]{1,0:T(8,128)(2,1)} %convolution_convert_fusion.6), channel_id=1, source_target_pairs={{0,1},{1,0},{2,3},{3,2},{4,5},{5,4},{6,7},{7,6},{8,9},{9,8},{10,11... | collective-permute-start | bytes 1769480 | tf_op jit(solution)/shard_map/ppermute | solution.py:46
  150.5 29.3 %collective-permute-start.31 = (f32[6,8,512]{2,1,0:T(8,128)}, f32[6,8,512]{2,1,0:T(8,128)}, u32[]{:S(2)}, u32[]{:S(2)}) collective-permute-start(f32[6,8,512]{2,1,0:T(8,128)} %add.389.refs_4_), channel_id=1, source_target_pairs={{2,0},{3,1},{6,4},{7,5},{10,8},{11,9},{14,12},{15,13},{18,16},{19,... | collective-permute-start | bytes 294920 | tf_op jit(solution)/shard_map/ppermute | solution.py:59
  154.9 26.6 %collective-permute-start.26 = (bf16[384,768]{1,0:T(8,128)(2,1)}, bf16[384,768]{1,0:T(8,128)(2,1)}, u32[]{:S(2)}, u32[]{:S(2)}) collective-permute-start(bf16[384,768]{1,0:T(8,128)(2,1)} %dynamic-slice_bitcast_fusion.1), channel_id=1, source_target_pairs={{0,4},{4,0},{8,12},{12,8},{16,20},{20,16},{24,28},{28,24},{1,5},{5... | collective-permute-start | bytes 1769480 | tf_op jit(solution)/shard_map/ppermute | solution.py:46
  168.3 14.8 %collective-permute-start.27 = (bf16[1,96,3072]{2,1,0:T(8,128)(2,1)}, bf16[1,96,3072]{2,1,0:T(8,128)(2,1)}, u32[]{:S(2)}, u32[]{:S(2)}) collective-permute-start(bf16[1,96,3072]{2,1,0:T(8,128)(2,1)} %constant_dynamic-slice_fusion.4), channel_id=1, source_target_pairs={{0,2},{1,3},{2,0},{3,1},{4,6},{5,7},{6,4},{7,5},{8,10},{9,11},{10,... | collective-permute-start | bytes 1769480 | tf_op jit(solution)/shard_map/ppermute | solution.py:46
  176.3 10.6 %collective-permute-start.32 = (f32[6,8,512]{2,1,0:T(8,128)}, f32[6,8,512]{2,1,0:T(8,128)S(1)}, u32[]{:S(2)}, u32[]{:S(2)}) collective-permute-start(f32[6,8,512]{2,1,0:T(8,128)} %add.389.refs_4_), channel_id=1, source_target_pairs={{0,1},{1,0},{2,3},{3,2},{4,5},{5,4},{6,7},{7,6},{8,9},{9,8},{10,11... | collective-permute-start | bytes 294920 | tf_op jit(solution)/shard_map/ppermute | solution.py:46
  179.8 24.5 %collective-permute-start.33 = (f32[6,8,512]{2,1,0:T(8,128)}, f32[6,8,512]{2,1,0:T(8,128)S(1)}, u32[]{:S(2)}, u32[]{:S(2)}) collective-permute-start(f32[6,8,512]{2,1,0:T(8,128)} %collective-permute-done.31.refs_5_), channel_id=1, source_target_pairs={{0,1},{1,0},{2,3},{3,2},{4,5},{5,4},{6,7},{7,6},{8,9},{9,8},{10,11... | collective-permute-start | bytes 294920 | tf_op jit(solution)/shard_map/ppermute | solution.py:46
  179.9 24.4 %collective-permute-start.29 = (bf16[512,768]{1,0:T(8,128)(2,1)S(1)}, bf16[512,768]{1,0:T(8,128)(2,1)S(1)}, u32[]{:S(2)}, u32[]{:S(2)}) collective-permute-start(bf16[512,768]{1,0:T(8,128)(2,1)S(1)} %copy-done.30), channel_id=1, source_target_pairs={{0,1},{1,0},{2,3},{3,2},{4,5},{5,4},{6,7},{7,6},{8,9},{9,8},{10,11... | collective-permute-start | bytes 2359304 | tf_op jit(solution)/shard_map/ppermute | solution.py:46
  181.6 25.3 %collective-permute-start.30 = (bf16[512,768]{1,0:T(8,128)(2,1)}, bf16[512,768]{1,0:T(8,128)(2,1)}, u32[]{:S(2)}, u32[]{:S(2)}) collective-permute-start(bf16[512,768]{1,0:T(8,128)(2,1)} %collective-permute-done.28.refs_1_), channel_id=1, source_target_pairs={{0,1},{1,0},{2,3},{3,2},{4,5},{5,4},{6,7},{7,6},{8,9},{9,8},{10,11... | collective-permute-start | bytes 2359304 | tf_op jit(solution)/shard_map/ppermute | solution.py:46
  185.8 51.5 %collective-permute-start.34 = (bf16[384,768]{1,0:T(8,128)(2,1)}, bf16[384,768]{1,0:T(8,128)(2,1)}, u32[]{:S(2)}, u32[]{:S(2)}) collective-permute-start(bf16[384,768]{1,0:T(8,128)(2,1)} %convolution_convert_fusion.5), channel_id=1, source_target_pairs={{0,1},{1,0},{2,3},{3,2},{4,5},{5,4},{6,7},{7,6},{8,9},{9,8},{10,11... | collective-permute-start | bytes 1769480 | tf_op jit(solution)/shard_map/ppermute | solution.py:46
  186.8 34.3 %collective-permute-start.36 = (bf16[192,768]{1,0:T(8,128)(2,1)}, bf16[192,768]{1,0:T(8,128)(2,1)}, u32[]{:S(2)}, u32[]{:S(2)}) collective-permute-start(bf16[192,768]{1,0:T(8,128)(2,1)} %get-tuple-element.201), channel_id=1, source_target_pairs={{0,8},{4,12},{8,0},{12,4},{16,24},{20,28},{24,16},{28,20},{1,9},{5... | collective-permute-start | bytes 884744 | tf_op jit(solution)/shard_map/ppermute | solution.py:46
  204.4 22.4 %collective-permute-start.37 = (bf16[192,768]{1,0:T(8,128)(2,1)S(1)}, bf16[192,768]{1,0:T(8,128)(2,1)}, u32[]{:S(2)}, u32[]{:S(2)}) collective-permute-start(bf16[192,768]{1,0:T(8,128)(2,1)S(1)} %get-tuple-element.203), channel_id=1, source_target_pairs={{0,16},{4,20},{8,24},{12,28},{16,0},{20,4},{24,8},{28,12},{1,17},{... | collective-permute-start | bytes 884744 | tf_op jit(solution)/shard_map/ppermute | solution.py:46
  205.0 21.8 %collective-permute-start.38 = (bf16[192,768]{1,0:T(8,128)(2,1)S(1)}, bf16[192,768]{1,0:T(8,128)(2,1)S(1)}, u32[]{:S(2)}, u32[]{:S(2)}) collective-permute-start(bf16[192,768]{1,0:T(8,128)(2,1)S(1)} %get-tuple-element.202), channel_id=1, source_target_pairs={{0,24},{4,28},{8,16},{12,20},{16,8},{20,12},{24,0},{28,4},{1,25},{... | collective-permute-start | bytes 884744 | tf_op jit(solution)/shard_map/ppermute | solution.py:46
  221.0 17.9 %collective-permute-start.35 = (bf16[384,768]{1,0:T(8,128)(2,1)S(1)}, bf16[384,768]{1,0:T(8,128)(2,1)S(1)}, u32[]{:S(2)}, u32[]{:S(2)}) collective-permute-start(bf16[384,768]{1,0:T(8,128)(2,1)S(1)} %convolution_convert_fusion.4), channel_id=1, source_target_pairs={{0,1},{1,0},{2,3},{3,2},{4,5},{5,4},{6,7},{7,6},{8,9},{9,8},{10,11... | collective-permute-start | bytes 1769480 | tf_op jit(solution)/shard_map/ppermute | solution.py:46
  228.0 34.6 %collective-permute-start.58 = (bf16[192,768]{1,0:T(8,128)(2,1)S(1)}, bf16[192,768]{1,0:T(8,128)(2,1)S(1)}, u32[]{:S(2)}, u32[]{:S(2)}) collective-permute-start(bf16[192,768]{1,0:T(8,128)(2,1)S(1)} %fusion.43), channel_id=1, source_target_pairs={{0,8},{4,12},{8,0},{12,4},{16,24},{20,28},{24,16},{28,20},{1,9},{5... | collective-permute-start | bytes 884744 | tf_op jit(solution)/shard_map/ppermute | solution.py:46
  234.8 27.9 %collective-permute-start.60 = (bf16[192,768]{1,0:T(8,128)(2,1)S(1)}, bf16[192,768]{1,0:T(8,128)(2,1)S(1)}, u32[]{:S(2)}, u32[]{:S(2)}) collective-permute-start(bf16[192,768]{1,0:T(8,128)(2,1)S(1)} %fusion.43), channel_id=1, source_target_pairs={{0,16},{4,20},{8,24},{12,28},{16,0},{20,4},{24,8},{28,12},{1,17},{... | collective-permute-start | bytes 884744 | tf_op jit(solution)/shard_map/ppermute | solution.py:46
  234.8 28.6 %collective-permute-start.59 = (bf16[192,768]{1,0:T(8,128)(2,1)S(1)}, bf16[192,768]{1,0:T(8,128)(2,1)}, u32[]{:S(2)}, u32[]{:S(2)}) collective-permute-start(bf16[192,768]{1,0:T(8,128)(2,1)S(1)} %fusion.43), channel_id=1, source_target_pairs={{0,24},{4,28},{8,16},{12,20},{16,8},{20,12},{24,0},{28,4},{1,25},{... | collective-permute-start | bytes 884744 | tf_op jit(solution)/shard_map/ppermute | solution.py:46
  241.0 29.9 %collective-permute-start.39 = (bf16[1,576,768]{2,1,0:T(8,128)(2,1)}, bf16[1,576,768]{2,1,0:T(8,128)(2,1)}, u32[]{:S(2)}, u32[]{:S(2)}) collective-permute-start(bf16[1,576,768]{2,1,0:T(8,128)(2,1)} %get-tuple-element.182), channel_id=1, source_target_pairs={{0,2},{1,3},{2,0},{3,1},{4,6},{5,7},{6,4},{7,5},{8,10},{9,11},{10,... | collective-permute-start | bytes 2654216 | tf_op jit(solution)/shard_map/ppermute | solution.py:46
  262.5 3.9 %collective-permute-start.40 = (bf16[384,768]{1,0:T(8,128)(2,1)S(1)}, bf16[384,768]{1,0:T(8,128)(2,1)S(1)}, u32[]{:S(2)}, u32[]{:S(2)}) collective-permute-start(bf16[384,768]{1,0:T(8,128)(2,1)S(1)} %convolution_convert_fusion.3), channel_id=1, source_target_pairs={{0,1},{1,0},{2,3},{3,2},{4,5},{5,4},{6,7},{7,6},{8,9},{9,8},{10,11... | collective-permute-start | bytes 1769480 | tf_op jit(solution)/shard_map/ppermute | solution.py:46
  267.8 12.1 %collective-permute-start.41 = (bf16[1,192,768]{2,1,0:T(8,128)(2,1)}, bf16[1,192,768]{2,1,0:T(8,128)(2,1)}, u32[]{:S(2)}, u32[]{:S(2)}) collective-permute-start(bf16[1,192,768]{2,1,0:T(8,128)(2,1)} %dynamic-slice_bitcast_fusion.3), channel_id=1, source_target_pairs={{0,2},{1,3},{2,0},{3,1},{4,6},{5,7},{6,4},{7,5},{8,10},{9,11},{10,... | collective-permute-start | bytes 884744 | tf_op jit(solution)/shard_map/ppermute | solution.py:46
  273.4 19.4 %collective-permute-start.42 = (bf16[192,768]{1,0:T(8,128)(2,1)}, bf16[192,768]{1,0:T(8,128)(2,1)S(1)}, u32[]{:S(2)}, u32[]{:S(2)}) collective-permute-start(bf16[192,768]{1,0:T(8,128)(2,1)} %dynamic-slice_bitcast_fusion.2), channel_id=1, source_target_pairs={{0,4},{4,0},{8,12},{12,8},{16,20},{20,16},{24,28},{28,24},{1,5},{5... | collective-permute-start | bytes 884744 | tf_op jit(solution)/shard_map/ppermute | solution.py:46
  279.9 3.7 %collective-permute-start.62 = (f32[12,768]{1,0:T(8,128)S(1)}, f32[12,768]{1,0:T(8,128)S(1)}, u32[]{:S(2)}, u32[]{:S(2)}) collective-permute-start(f32[12,768]{1,0:T(8,128)S(1)} %concatenate.106), channel_id=1, source_target_pairs={{0,1},{1,0},{2,3},{3,2},{4,5},{5,4},{6,7},{7,6},{8,9},{9,8},{10,11... | collective-permute-start | bytes 110600 | tf_op jit(solution)/shard_map/ppermute | solution.py:46
  282.2 10.5 %collective-permute-start.43 = (bf16[192,768]{1,0:T(8,128)(2,1)S(1)}, bf16[192,768]{1,0:T(8,128)(2,1)S(1)}, u32[]{:S(2)}, u32[]{:S(2)}) collective-permute-start(bf16[192,768]{1,0:T(8,128)(2,1)S(1)} %bitcast.202), channel_id=1, source_target_pairs={{0,4},{4,0},{8,12},{12,8},{16,20},{20,16},{24,28},{28,24},{1,5},{5... | collective-permute-start | bytes 884744 | tf_op jit(solution)/shard_map/ppermute | solution.py:46
  283.6 9.0 %collective-permute-start.63 = (f32[12,768]{1,0:T(8,128)S(1)}, f32[12,768]{1,0:T(8,128)S(1)}, u32[]{:S(2)}, u32[]{:S(2)}) collective-permute-start(f32[12,768]{1,0:T(8,128)S(1)} %add.417), channel_id=1, source_target_pairs={{0,4},{4,0},{8,12},{12,8},{16,20},{20,16},{24,28},{28,24},{1,5},{5... | collective-permute-start | bytes 110600 | tf_op jit(solution)/shard_map/ppermute | solution.py:46
  291.2 46.4 %collective-permute-start.61 = (bf16[768,768]{1,0:T(8,128)(2,1)S(1)}, bf16[768,768]{1,0:T(8,128)(2,1)S(1)}, u32[]{:S(2)}, u32[]{:S(2)}) collective-permute-start(bf16[768,768]{1,0:T(8,128)(2,1)S(1)} %copy-done.59), channel_id=1, source_target_pairs={{0,4},{4,0},{8,12},{12,8},{16,20},{20,16},{24,28},{28,24},{1,5},{5... | collective-permute-start | bytes 3538952 | tf_op jit(solution)/shard_map/ppermute | solution.py:46
  292.7 25.4 %collective-permute-start.64 = (f32[12,768]{1,0:T(8,128)S(1)}, f32[12,768]{1,0:T(8,128)S(1)}, u32[]{:S(2)}, u32[]{:S(2)}) collective-permute-start(f32[12,768]{1,0:T(8,128)S(1)} %add.418), channel_id=1, source_target_pairs={{0,2},{1,3},{2,0},{3,1},{4,6},{5,7},{6,4},{7,5},{8,10},{9,11},{10,... | collective-permute-start | bytes 110600 | tf_op jit(solution)/shard_map/ppermute | solution.py:46
  293.2 10.9 %collective-permute-start.44 = (bf16[48,768]{1,0:T(8,128)(2,1)S(1)}, bf16[48,768]{1,0:T(8,128)(2,1)S(1)}, u32[]{:S(2)}, u32[]{:S(2)}) collective-permute-start(bf16[48,768]{1,0:T(8,128)(2,1)S(1)} %get-tuple-element.235), channel_id=1, source_target_pairs={{0,8},{4,12},{8,0},{12,4},{16,24},{20,28},{24,16},{28,20},{1,9},{5... | collective-permute-start | bytes 221192 | tf_op jit(solution)/shard_map/ppermute | solution.py:46
  301.6 8.2 %collective-permute-start.45 = (bf16[48,768]{1,0:T(8,128)(2,1)S(1)}, bf16[48,768]{1,0:T(8,128)(2,1)S(1)}, u32[]{:S(2)}, u32[]{:S(2)}) collective-permute-start(bf16[48,768]{1,0:T(8,128)(2,1)S(1)} %get-tuple-element.237), channel_id=1, source_target_pairs={{0,16},{4,20},{8,24},{12,28},{16,0},{20,4},{24,8},{28,12},{1,17},{... | collective-permute-start | bytes 221192 | tf_op jit(solution)/shard_map/ppermute | solution.py:46
  301.6 8.2 %collective-permute-start.46 = (bf16[48,768]{1,0:T(8,128)(2,1)S(1)}, bf16[48,768]{1,0:T(8,128)(2,1)S(1)}, u32[]{:S(2)}, u32[]{:S(2)}) collective-permute-start(bf16[48,768]{1,0:T(8,128)(2,1)S(1)} %get-tuple-element.236), channel_id=1, source_target_pairs={{0,24},{4,28},{8,16},{12,20},{16,8},{20,12},{24,0},{28,4},{1,25},{... | collective-permute-start | bytes 221192 | tf_op jit(solution)/shard_map/ppermute | solution.py:46
  304.1 6.9 %collective-permute-start.48 = (bf16[48,768]{1,0:T(8,128)(2,1)S(1)}, bf16[48,768]{1,0:T(8,128)(2,1)S(1)}, u32[]{:S(2)}, u32[]{:S(2)}) collective-permute-start(bf16[48,768]{1,0:T(8,128)(2,1)S(1)} %get-tuple-element.232), channel_id=1, source_target_pairs={{0,8},{4,12},{8,0},{12,4},{16,24},{20,28},{24,16},{28,20},{1,9},{5... | collective-permute-start | bytes 221192 | tf_op jit(solution)/shard_map/ppermute | solution.py:46
  309.8 7.0 %collective-permute-start.49 = (bf16[48,768]{1,0:T(8,128)(2,1)S(1)}, bf16[48,768]{1,0:T(8,128)(2,1)S(1)}, u32[]{:S(2)}, u32[]{:S(2)}) collective-permute-start(bf16[48,768]{1,0:T(8,128)(2,1)S(1)} %get-tuple-element.234), channel_id=1, source_target_pairs={{0,16},{4,20},{8,24},{12,28},{16,0},{20,4},{24,8},{28,12},{1,17},{... | collective-permute-start | bytes 221192 | tf_op jit(solution)/shard_map/ppermute | solution.py:46
  309.8 7.0 %collective-permute-start.50 = (bf16[48,768]{1,0:T(8,128)(2,1)S(1)}, bf16[48,768]{1,0:T(8,128)(2,1)S(1)}, u32[]{:S(2)}, u32[]{:S(2)}) collective-permute-start(bf16[48,768]{1,0:T(8,128)(2,1)S(1)} %get-tuple-element.233), channel_id=1, source_target_pairs={{0,24},{4,28},{8,16},{12,20},{16,8},{20,12},{24,0},{28,4},{1,25},{... | collective-permute-start | bytes 221192 | tf_op jit(solution)/shard_map/ppermute | solution.py:46
  311.0 9.6 %collective-permute-start.52 = (bf16[48,768]{1,0:T(8,128)(2,1)S(1)}, bf16[48,768]{1,0:T(8,128)(2,1)S(1)}, u32[]{:S(2)}, u32[]{:S(2)}) collective-permute-start(bf16[48,768]{1,0:T(8,128)(2,1)S(1)} %fusion.66), channel_id=1, source_target_pairs={{0,8},{4,12},{8,0},{12,4},{16,24},{20,28},{24,16},{28,20},{1,9},{5... | collective-permute-start | bytes 221192 | tf_op jit(solution)/shard_map/ppermute | solution.py:46
  316.8 7.0 %collective-permute-start.51 = (bf16[48,768]{1,0:T(8,128)(2,1)S(1)}, bf16[48,768]{1,0:T(8,128)(2,1)S(1)}, u32[]{:S(2)}, u32[]{:S(2)}) collective-permute-start(bf16[48,768]{1,0:T(8,128)(2,1)S(1)} %fusion.66), channel_id=1, source_target_pairs={{0,16},{4,20},{8,24},{12,28},{16,0},{20,4},{24,8},{28,12},{1,17},{... | collective-permute-start | bytes 221192 | tf_op jit(solution)/shard_map/ppermute | solution.py:46
  316.8 7.8 %collective-permute-start.47 = (bf16[48,768]{1,0:T(8,128)(2,1)S(1)}, bf16[48,768]{1,0:T(8,128)(2,1)S(1)}, u32[]{:S(2)}, u32[]{:S(2)}) collective-permute-start(bf16[48,768]{1,0:T(8,128)(2,1)S(1)} %fusion.66), channel_id=1, source_target_pairs={{0,24},{4,28},{8,16},{12,20},{16,8},{20,12},{24,0},{28,4},{1,25},{... | collective-permute-start | bytes 221192 | tf_op jit(solution)/shard_map/ppermute | solution.py:46
  318.1 7.2 %collective-permute-start.56 = (bf16[48,768]{1,0:T(8,128)(2,1)S(1)}, bf16[48,768]{1,0:T(8,128)(2,1)S(1)}, u32[]{:S(2)}, u32[]{:S(2)}) collective-permute-start(bf16[48,768]{1,0:T(8,128)(2,1)S(1)} %fusion.63), channel_id=1, source_target_pairs={{0,8},{4,12},{8,0},{12,4},{16,24},{20,28},{24,16},{28,20},{1,9},{5... | collective-permute-start | bytes 221192 | tf_op jit(solution)/shard_map/ppermute | solution.py:46
  320.7 7.1 %collective-permute-start.55 = (bf16[48,768]{1,0:T(8,128)(2,1)S(1)}, bf16[48,768]{1,0:T(8,128)(2,1)S(1)}, u32[]{:S(2)}, u32[]{:S(2)}) collective-permute-start(bf16[48,768]{1,0:T(8,128)(2,1)S(1)} %fusion.63), channel_id=1, source_target_pairs={{0,16},{4,20},{8,24},{12,28},{16,0},{20,4},{24,8},{28,12},{1,17},{... | collective-permute-start | bytes 221192 | tf_op jit(solution)/shard_map/ppermute | solution.py:46
  323.8 6.2 %collective-permute-start.54 = (bf16[48,768]{1,0:T(8,128)(2,1)S(1)}, bf16[48,768]{1,0:T(8,128)(2,1)S(1)}, u32[]{:S(2)}, u32[]{:S(2)}) collective-permute-start(bf16[48,768]{1,0:T(8,128)(2,1)S(1)} %fusion.63), channel_id=1, source_target_pairs={{0,24},{4,28},{8,16},{12,20},{16,8},{20,12},{24,0},{28,4},{1,25},{... | collective-permute-start | bytes 221192 | tf_op jit(solution)/shard_map/ppermute | solution.py:46
  324.7 9.3 %collective-permute-start.53 = (bf16[192,768]{1,0:T(8,128)(2,1)S(1)}, bf16[192,768]{1,0:T(8,128)(2,1)S(1)}, u32[]{:S(2)}, u32[]{:S(2)}) collective-permute-start(bf16[192,768]{1,0:T(8,128)(2,1)S(1)} %pad_maximum_fusion.13), channel_id=1, source_target_pairs={{0,4},{4,0},{8,12},{12,8},{16,20},{20,16},{24,28},{28,24},{1,5},{5... | collective-permute-start | bytes 884744 | tf_op jit(solution)/shard_map/ppermute | solution.py:46
  330.0 7.2 %collective-permute-start.57 = (bf16[192,768]{1,0:T(8,128)(2,1)S(1)}, bf16[192,768]{1,0:T(8,128)(2,1)S(1)}, u32[]{:S(2)}, u32[]{:S(2)}) collective-permute-start(bf16[192,768]{1,0:T(8,128)(2,1)S(1)} %pad_maximum_fusion.14), channel_id=1, source_target_pairs={{0,4},{4,0},{8,12},{12,8},{16,20},{20,16},{24,28},{28,24},{1,5},{5... | collective-permute-start | bytes 884744 | tf_op jit(solution)/shard_map/ppermute | solution.py:46
  337.6 5.6 %collective-permute-start.65 = (f32[12,768]{1,0:T(8,128)S(1)}, f32[12,768]{1,0:T(8,128)S(1)}, u32[]{:S(2)}, u32[]{:S(2)}) collective-permute-start(f32[12,768]{1,0:T(8,128)S(1)} %add_add_fusion.2), channel_id=1, source_target_pairs={{0,8},{4,12},{8,0},{12,4},{16,24},{20,28},{24,16},{28,20},{1,9},{5... | collective-permute-start | bytes 110600 | tf_op jit(solution)/shard_map/ppermute | solution.py:46
  343.2 5.0 %collective-permute-start.66 = (f32[12,768]{1,0:T(8,128)S(1)}, f32[12,768]{1,0:T(8,128)S(1)}, u32[]{:S(2)}, u32[]{:S(2)}) collective-permute-start(f32[12,768]{1,0:T(8,128)S(1)} %add.423), channel_id=1, source_target_pairs={{0,16},{4,20},{8,24},{12,28},{16,0},{20,4},{24,8},{28,12},{1,17},{... | collective-permute-start | bytes 110600 | tf_op jit(solution)/shard_map/ppermute | solution.py:46
  (93 other events, 644.3 us)
